TPU v7x, 128 devices: a whole 4x4x4 slice. The times are simulated.
128 devices in a mesh: ctx: 64 (over x, y, z_hi, core), kv: 2 (over z_lo).
Axes of the slice: x: 4, y: 4, z: 4 (z_hi: 2, z_lo: 2; z = z_hi * 2 + z_lo), core: 2. Of those that a mesh axis runs over, the one named last changes fastest.
Arguments:
- query_rows: bfloat16 [8192, 16, 128], P('ctx', 'kv'), may hold values from -5.5 to 5.5
- key_rows: bfloat16 [8192, 2, 128], P('ctx', 'kv'), may hold values from -5.5 to 5.5
- value_rows: bfloat16 [8192, 2, 128], P('ctx', 'kv'), may hold values from -6 to 6
- attn_out: bfloat16 [8192, 16, 128], P('ctx', 'kv'), may hold values from -4 to 4
- attn_grad: bfloat16 [8192, 16, 128], P('ctx', 'kv'), may hold values from -6 to 6
- log_total: float32 [8192, 16], P('ctx', 'kv'), may hold values from -400 to 400, as said below
- stretch_order: int32 [128], replicated, may hold values from 0 to 127, as said below
- moe_rows: bfloat16 [8192, 2048], P(('ctx', 'kv')), may hold values from -6 to 6
- moe_grad: bfloat16 [8192, 2048], P(('ctx', 'kv')), may hold values from -3 to 3
- expert_ids: int32 [8192, 8], P(('ctx', 'kv')), may hold values from 0 to 127, all different within a row; in each aligned block of 64 rows (0 to 63, 64 to 127, ...) at most 5 rows name the same one
- gate_prob: bfloat16 [8192, 8], P(('ctx', 'kv')), may hold values from 0.049804688 to 0.29882812
- gate_weight: bfloat16 [128, 2048, 768], P(('ctx', 'kv')), may hold values from -0.125 to 0.125
- up_weight: bfloat16 [128, 2048, 768], P(('ctx', 'kv')), may hold values from -0.125 to 0.125
- down_weight: bfloat16 [128, 768, 2048], P(('ctx', 'kv')), may hold values from -0.21875 to 0.21875
Outputs:
- d_query: bfloat16 [8192, 16, 128], P('ctx', 'kv')
- d_key: bfloat16 [8192, 2, 128], P('ctx', 'kv')
- d_value: bfloat16 [8192, 2, 128], P('ctx', 'kv')
- d_rows: bfloat16 [8192, 2048], P(('ctx', 'kv'))
- d_gates: bfloat16 [8192, 8], P(('ctx', 'kv'))
- grad_gate: bfloat16 [128, 2048, 768], P(('ctx', 'kv'))
- grad_up: bfloat16 [128, 2048, 768], P(('ctx', 'kv'))
- grad_down: bfloat16 [128, 768, 2048], P(('ctx', 'kv'))
Inputs may be any that keep to these rules, and one draw needn't show every extreme that they name: `stretch_order`: entries 2 d and 2 d + 1 are the stretches stored by context index d: a stretch c below 64 and 127 - c; every stretch appears once. `expert_ids`: each row names 8 different experts. Among the 64 rows of one device no expert is named more than 5 times, a bound that some block reaches. `log_total`: the log of the sum of exp(scores) over the allowed keys of the row, from the forward pass.
All inputs are finite; a program needn't handle non-finite values.
Results may differ from a plain program's by a relative error of at most 0.013.
Values may be sent and summed in bfloat16 or wider, within the bound.
A program may use at most 128 MiB of HBM per device.

v0:
```python
import math

import jax
import jax.numpy as jnp
from jax import lax
from jax.sharding import PartitionSpec as P


def shifted(value, axis, steps):
    count = lax.axis_size(axis)
    pairs = [(source, (source + steps) % count) for source in range(count)]
    return lax.ppermute(value, axis, pairs)


def block_positions(stretch_order, first_row, row_count, stretch_len):
    row_ids = first_row + jnp.arange(row_count, dtype=jnp.int32)
    stretch_idx = row_ids // stretch_len
    stretch_hit = (
        stretch_idx[:, None] == jnp.arange(stretch_order.shape[0], dtype=jnp.int32)[None, :]
    )
    starts = jnp.sum(jnp.where(stretch_hit, stretch_order[None, :], 0), axis=1)
    return starts * stretch_len + row_ids % stretch_len


def tile_grads(queries, grads_out, row_log, deltas, query_pos, key_block, value_block, key_pos):
    score_scale = 1.0 / math.sqrt(queries.shape[-1])
    keys_flat = key_block[:, 0, :]
    values_flat = value_block[:, 0, :]
    scores = (
        jnp.einsum("qid,kd->iqk", queries, keys_flat, preferred_element_type=jnp.float32)
        * score_scale
    )
    allowed = (key_pos[None, :] <= query_pos[:, None])[None]
    attn_probs = jnp.where(
        allowed, jnp.exp(jnp.where(allowed, scores - row_log[:, :, None], 0.0)), 0.0
    )
    probs_low = attn_probs.astype(jnp.bfloat16)
    value_grad = jnp.einsum("iqk,qid->kd", probs_low, grads_out, preferred_element_type=jnp.float32)
    prob_grad = jnp.einsum(
        "qid,kd->iqk", grads_out, values_flat, preferred_element_type=jnp.float32
    )
    score_grad = (attn_probs * (prob_grad - deltas[:, :, None])).astype(jnp.bfloat16)
    query_grad = (
        jnp.einsum("iqk,kd->qid", score_grad, keys_flat, preferred_element_type=jnp.float32)
        * score_scale
    )
    key_grad = (
        jnp.einsum("iqk,qid->kd", score_grad, queries, preferred_element_type=jnp.float32)
        * score_scale
    )
    return (query_grad, key_grad[:, None, :], value_grad[:, None, :])


def pass_on(key_acc, value_acc):
    return shifted((key_acc, value_acc), "ctx", 1)


def expert_grads(rows_in, grads_in, gates_in, gate_mat, up_mat, down_mat):
    contract_rows = (((0,), (0,)), ((), ()))
    contract_cols = (((1,), (1,)), ((), ()))
    gate_act = jnp.dot(rows_in, gate_mat, preferred_element_type=jnp.float32)
    up_act = jnp.dot(rows_in, up_mat, preferred_element_type=jnp.float32)
    gate_sig = jax.nn.sigmoid(gate_act)
    hidden = (gate_act * gate_sig * up_act).astype(jnp.bfloat16)
    projected = lax.dot_general(
        grads_in, down_mat, contract_cols, preferred_element_type=jnp.float32
    )
    slot_gate = jnp.sum(projected * hidden.astype(jnp.float32), axis=1).astype(jnp.bfloat16)
    gate_col = gates_in.astype(jnp.float32)[:, None]
    hidden_grad = gate_col * projected
    gate_grad = (hidden_grad * up_act * gate_sig * (1.0 + gate_act * (1.0 - gate_sig))).astype(
        jnp.bfloat16
    )
    up_grad = (hidden_grad * gate_act * gate_sig).astype(jnp.bfloat16)
    slot_rows = (
        lax.dot_general(gate_grad, gate_mat, contract_cols, preferred_element_type=jnp.float32)
        + lax.dot_general(up_grad, up_mat, contract_cols, preferred_element_type=jnp.float32)
    ).astype(jnp.bfloat16)
    scaled_grads = (gate_col * grads_in.astype(jnp.float32)).astype(jnp.bfloat16)
    gate_sum = lax.dot_general(
        rows_in, gate_grad, contract_rows, preferred_element_type=jnp.float32
    )
    up_sum = lax.dot_general(rows_in, up_grad, contract_rows, preferred_element_type=jnp.float32)
    down_sum = lax.dot_general(
        hidden, scaled_grads, contract_rows, preferred_element_type=jnp.float32
    )
    return (slot_rows, slot_gate, gate_sum, up_sum, down_sum)


def shards(
    query_rows,
    key_rows,
    value_rows,
    attn_out,
    attn_grad,
    log_total,
    stretch_order,
    moe_rows,
    moe_grad,
    expert_ids,
    gate_prob,
    gate_weight,
    up_weight,
    down_weight,
):
    tok_rows = query_rows.shape[0]
    group_size = query_rows.shape[1]
    head_size = query_rows.shape[2]
    stretch_len = tok_rows // 2
    cycle_size = lax.axis_size("ctx")
    here_index = lax.axis_index("ctx")
    query_pos = block_positions(stretch_order, here_index * tok_rows, tok_rows, stretch_len)
    row_log = jnp.transpose(log_total, (1, 0))
    deltas = jnp.einsum("qid,qid->iq", attn_grad, attn_out, preferred_element_type=jnp.float32)
    zero_query = jnp.zeros((tok_rows, group_size, head_size), jnp.float32)
    zero_keys = jnp.zeros(key_rows.shape, jnp.float32)

    def turn(turn_index, cycle_state):
        key_block, value_block, key_acc, value_acc, query_acc = cycle_state
        anchor = (here_index - turn_index) % cycle_size
        key_pos = block_positions(stretch_order, anchor * tok_rows, tok_rows, stretch_len)
        query_grad, key_grad, value_grad = tile_grads(
            query_rows, attn_grad, row_log, deltas, query_pos, key_block, value_block, key_pos
        )
        key_block, value_block = shifted((key_block, value_block), "ctx", 1)
        key_acc, value_acc = pass_on(key_acc + key_grad, value_acc + value_grad)
        return (key_block, value_block, key_acc, value_acc, query_acc + query_grad)

    key_block, value_block, key_acc, value_acc, query_acc = lax.fori_loop(
        0, cycle_size - 1, turn, (key_rows, value_rows, zero_keys, zero_keys, zero_query)
    )
    anchor = (here_index + 1) % cycle_size
    key_pos = block_positions(stretch_order, anchor * tok_rows, tok_rows, stretch_len)
    query_grad, key_grad, value_grad = tile_grads(
        query_rows, attn_grad, row_log, deltas, query_pos, key_block, value_block, key_pos
    )
    query_acc = query_acc + query_grad
    key_acc, value_acc = pass_on(key_acc + key_grad, value_acc + value_grad)
    rows_here = moe_rows.shape[0]
    model_width = moe_rows.shape[1]
    top_count = expert_ids.shape[1]
    ctx_count = lax.axis_size("ctx")
    kv_count = lax.axis_size("kv")
    experts = ctx_count * kv_count
    capacity = max(2, 5 * rows_here * top_count // (4 * experts))
    flat_ids = expert_ids.reshape(-1)
    expert_hits = (flat_ids[:, None] == jnp.arange(experts, dtype=jnp.int32)[None, :]).astype(
        jnp.int32
    )
    rank_in = jnp.sum((jnp.cumsum(expert_hits, axis=0) - expert_hits) * expert_hits, axis=1)
    slot_of = flat_ids * capacity + rank_in
    owner_row = jnp.arange(rows_here * top_count, dtype=jnp.int32) // top_count
    source_of = jnp.full((experts * capacity,), rows_here, jnp.int32).at[slot_of].set(owner_row)
    zero_row = jnp.zeros((1, model_width), jnp.bfloat16)
    send_rows = jnp.concatenate([moe_rows, zero_row])[source_of]
    send_grads = jnp.concatenate([moe_grad, zero_row])[source_of]
    send_gates = (
        jnp.zeros((experts * capacity,), jnp.bfloat16).at[slot_of].set(gate_prob.reshape(-1))
    )
    got_rows, got_grads, got_gates = (
        lax.all_to_all(
            send_rows.reshape(experts, capacity, model_width),
            ("ctx", "kv"),
            split_axis=0,
            concat_axis=0,
            tiled=True,
        ),
        lax.all_to_all(
            send_grads.reshape(experts, capacity, model_width),
            ("ctx", "kv"),
            split_axis=0,
            concat_axis=0,
            tiled=True,
        ),
        lax.all_to_all(
            send_gates.reshape(experts, capacity),
            ("ctx", "kv"),
            split_axis=0,
            concat_axis=0,
            tiled=True,
        ),
    )
    slot_rows, slot_gate, gate_sum, up_sum, down_sum = expert_grads(
        got_rows.reshape(-1, model_width),
        got_grads.reshape(-1, model_width),
        got_gates.reshape(-1),
        gate_weight[0],
        up_weight[0],
        down_weight[0],
    )
    back_rows, back_gates = (
        lax.all_to_all(
            slot_rows.reshape(experts, capacity, model_width),
            ("ctx", "kv"),
            split_axis=0,
            concat_axis=0,
            tiled=True,
        ),
        lax.all_to_all(
            slot_gate.reshape(experts, capacity),
            ("ctx", "kv"),
            split_axis=0,
            concat_axis=0,
            tiled=True,
        ),
    )
    picked_rows = back_rows.reshape(-1, model_width)[slot_of].reshape(
        rows_here, top_count, model_width
    )
    d_rows = jnp.sum(picked_rows.astype(jnp.float32), axis=1).astype(jnp.bfloat16)
    d_gates = back_gates.reshape(-1)[slot_of].reshape(rows_here, top_count)
    return (
        query_acc.astype(jnp.bfloat16),
        key_acc.astype(jnp.bfloat16),
        value_acc.astype(jnp.bfloat16),
        d_rows,
        d_gates,
        gate_sum[None].astype(jnp.bfloat16),
        up_sum[None].astype(jnp.bfloat16),
        down_sum[None].astype(jnp.bfloat16),
    )


def solution(mesh):
    placed = (
        P("ctx", "kv", None),
        P("ctx", "kv", None),
        P("ctx", "kv", None),
        P("ctx", "kv", None),
        P("ctx", "kv", None),
        P("ctx", "kv"),
        P(),
        P(("ctx", "kv"), None),
        P(("ctx", "kv"), None),
        P(("ctx", "kv"), None),
        P(("ctx", "kv"), None),
        P(("ctx", "kv"), None, None),
        P(("ctx", "kv"), None, None),
        P(("ctx", "kv"), None, None),
    )
    return jax.shard_map(
        shards,
        mesh=mesh,
        in_specs=placed,
        out_specs=(
            P("ctx", "kv", None),
            P("ctx", "kv", None),
            P("ctx", "kv", None),
            P(("ctx", "kv"), None),
            P(("ctx", "kv"), None),
            P(("ctx", "kv"), None, None),
            P(("ctx", "kv"), None, None),
            P(("ctx", "kv"), None, None),
        ),
        check_vma=False,
    )
```

profile of v0, /device:TPU:0, one launch (start us, length us, event | category | flops | bytes accessed | tf_op | source)
XLA Modules:
  0.0 1351.7 jit_solution(7773151553250314033)
XLA Ops:
  11.6 11.1 all-to-all-start
  30.2 5.5 reshape.300
  36.3 10.3 all-to-all-start.2
  55.4 5.5 reshape.298
  61.8 37.4 %all-to-all-done.2 = bf16[128,5,2048]{2,1,0:T(8,128)(2,1)} async-done(((bf16[128,5,2048]{2,1,0:T(8,128)(2,1)}), bf16[128,5,2048]{2,1,0:T(8,128)(2,1)}, u32[]{:S(2)}, u32[]{:S(2)}) %all-to-all-start.2) | async-done | bytes 2621472 | tf_op jit(solution)/shard_map/all_to_all | solution.py:161
  99.2 6.1 all-to-all-start.1
  105.9 1079.6 %while.24 = (s32[]{:T(128)}, bf16[128,1,128]{2,0,1:T(8,128)(2,1)}, bf16[128,1,128]{2,0,1:T(8,128)(2,1)}, f32[128,1,128]{2,0,1:T(8,128)}, f32[128,1,128]{2,0,1:T(...) while((s32[]{:T(128)}, bf16[128,1,128]{2,0,1:T(8,128)(2,1)}, ...), condition=%wide.region_3.4_spmd.clone, body=%wide.region_1.3_spmd.clone.sunk | while | flops 169332368 | bytes 6828536 | solution.py:129
  118.1 40.4 %collective-permute-done = bf16[128,1,128]{2,0,1:T(8,128)(2,1)} collective-permute-done((bf16[128,1,128]{2,0,1:T(8,128)(2,1)S(1)}, bf16[128,1,128]{2,0,1:T(8,128)(2,1)}, u32[]{:S(2)}, u32[]{:S(2)}) %collective-permute-start) | collective-permute-done | bytes 32800 | tf_op jit(solution)/shard_map/while/body/eval_jaxpr/ppermute | solution.py:12
  220.4 5.1 collective-permute-done.2
  253.5 5.1 collective-permute-done.2
  286.5 5.1 collective-permute-done.2
  385.8 5.1 collective-permute-done.2
  518.1 5.1 collective-permute-done.2
  617.3 5.1 collective-permute-done.2
  650.4 5.1 collective-permute-done.2
  749.6 5.1 collective-permute-done.2
  782.7 5.1 collective-permute-done.2
  882.0 5.1 collective-permute-done.2
  1014.3 5.1 collective-permute-done.2
  1146.6 5.1 collective-permute-done.2
  1188.8 5.6 reshape.301
  1194.4 5.4 fusion.21
  1203.2 5.6 reshape.299
  1208.8 8.1 multiply_reduce_fusion
  1222.3 14.8 %all-to-all-start.4 = ((bf16[128,1,5]{2,1,0:T(2,128)(2,1)}), bf16[128,1,5]{2,1,0:T(2,128)(2,1)S(1)}, u32[]{:S(2)}, u32[]{:S(2)}) async-start(bf16[128,1,5]{2,1,0:T(2,128)(2,1)} %convert_element_type.134), calls=%async_computation.4 | async-start | bytes 131072 | tf_op jit(solution)/shard_map/all_to_all | solution.py:199
  1237.1 7.5 add_convert_fusion
  1244.6 5.5 reshape.302
  1250.1 10.3 all-to-all-start.3
  1272.7 40.4 %collective-permute-done.5 = bf16[128,1,128]{2,0,1:T(8,128)(2,1)S(1)} collective-permute-done((bf16[128,1,128]{2,0,1:T(8,128)(2,1)}, bf16[128,1,128]{2,0,1:T(8,128)(2,1)S(1)}, u32[]{:S(2)}, u32[]{:S(2)}) %collective-permute-start.5) | collective-permute-done | bytes 32800 | tf_op jit(solution)/shard_map/ppermute | solution.py:12
  1313.6 6.3 fusion.28
  1332.9 5.6 reshape.303
  1338.5 7.4 gather_fusion.2
  (1408 shorter events, 1048.3 us)
Async XLA Ops:
  11.6 24.1 %all-to-all-start = ((bf16[128,1,5]{2,1,0:T(2,128)(2,1)}), bf16[128,1,5]{2,1,0:T(2,128)(2,1)S(1)}, u32[]{:S(2)}, u32[]{:S(2)}) async-start(bf16[128,1,5]{2,1,0:T(2,128)(2,1)} %all_to_all.25), calls=%async_computation | async-start | bytes 131072 | tf_op jit(solution)/shard_map/all_to_all | solution.py:175
  36.3 62.8 %all-to-all-start.2 = ((bf16[128,5,2048]{2,1,0:T(8,128)(2,1)}), bf16[128,5,2048]{2,1,0:T(8,128)(2,1)}, u32[]{:S(2)}, u32[]{:S(2)}) async-start(bf16[128,5,2048]{2,1,0:T(8,128)(2,1)} %reshape.300), calls=%async_computation.2 | async-start | bytes 8388608 | tf_op jit(solution)/shard_map/all_to_all | solution.py:161
  99.2 1104.0 %all-to-all-start.1 = ((bf16[128,5,2048]{2,1,0:T(8,128)(2,1)}), bf16[128,5,2048]{2,1,0:T(8,128)(2,1)}, u32[]{:S(2)}, u32[]{:S(2)}) async-start(bf16[128,5,2048]{2,1,0:T(8,128)(2,1)} %reshape.298), calls=%async_computation.1 | async-start | bytes 8388608 | tf_op jit(solution)/shard_map/all_to_all | solution.py:168
  106.7 51.8 %collective-permute-start = (bf16[128,1,128]{2,0,1:T(8,128)(2,1)S(1)}, bf16[128,1,128]{2,0,1:T(8,128)(2,1)}, u32[]{:S(2)}, u32[]{:S(2)}) collective-permute-start(bf16[128,1,128]{2,0,1:T(8,128)(2,1)S(1)} %copy.118), channel_id=1, source_target_pairs={{0,2},{2,4},{4,6},{6,8},{8,10},{10,12},{12,14},{14,16},{16,18},{18... | collective-permute-start | bytes 98312 | tf_op jit(solution)/shard_map/while/body/eval_jaxpr/ppermute | solution.py:12
  107.4 51.4 %collective-permute-start.1 = (bf16[128,1,128]{2,0,1:T(8,128)(2,1)S(1)}, bf16[128,1,128]{2,0,1:T(8,128)(2,1)}, u32[]{:S(2)}, u32[]{:S(2)}) collective-permute-start(bf16[128,1,128]{2,0,1:T(8,128)(2,1)S(1)} %copy.119), channel_id=1, source_target_pairs={{0,2},{2,4},{4,6},{6,8},{8,10},{10,12},{12,14},{14,16},{16,18},{18... | collective-permute-start | bytes 98312 | tf_op jit(solution)/shard_map/while/body/eval_jaxpr/ppermute | solution.py:12
  115.0 44.5 %collective-permute-start.2 = (f32[128,1,128]{2,0,1:T(8,128)}, f32[128,1,128]{2,0,1:T(8,128)}, u32[]{:S(2)}, u32[]{:S(2)}) collective-permute-start(f32[128,1,128]{2,0,1:T(8,128)} %fusion.117), channel_id=1, source_target_pairs={{0,2},{2,4},{4,6},{6,8},{8,10},{10,12},{12,14},{14,16},{16,18},{18... | collective-permute-start | bytes 196616 | tf_op jit(solution)/shard_map/while/body/eval_jaxpr/ppermute | solution.py:12
  116.0 44.1 %collective-permute-start.3 = (f32[128,1,128]{2,0,1:T(8,128)}, f32[128,1,128]{2,0,1:T(8,128)S(1)}, u32[]{:S(2)}, u32[]{:S(2)}) collective-permute-start(f32[128,1,128]{2,0,1:T(8,128)} %fusion.118), channel_id=1, source_target_pairs={{0,2},{2,4},{4,6},{6,8},{8,10},{10,12},{12,14},{14,16},{16,18},{18... | collective-permute-start | bytes 196616 | tf_op jit(solution)/shard_map/while/body/eval_jaxpr/ppermute | solution.py:12
  160.8 10.3 collective-permute-start
  166.1 9.7 collective-permute-start.2
  182.7 9.7 collective-permute-start.2
  215.8 9.7 collective-permute-start.2
  248.8 9.7 collective-permute-start.2
  315.0 9.7 collective-permute-start.2
  348.1 9.7 collective-permute-start.2
  381.1 9.7 collective-permute-start.2
  447.3 9.7 collective-permute-start.2
  480.4 9.7 collective-permute-start.2
  513.5 9.7 collective-permute-start.2
  579.6 9.7 collective-permute-start.2
  612.7 9.7 collective-permute-start.2
  645.8 9.7 collective-permute-start.2
  678.8 9.7 collective-permute-start.2
  711.9 9.7 collective-permute-start.2
  745.0 9.7 collective-permute-start.2
  778.1 9.7 collective-permute-start.2
  811.2 9.7 collective-permute-start.2
  844.2 9.7 collective-permute-start.2
  877.3 9.7 collective-permute-start.2
  1222.3 27.7 %all-to-all-start.4 = ((bf16[128,1,5]{2,1,0:T(2,128)(2,1)}), bf16[128,1,5]{2,1,0:T(2,128)(2,1)S(1)}, u32[]{:S(2)}, u32[]{:S(2)}) async-start(bf16[128,1,5]{2,1,0:T(2,128)(2,1)} %convert_element_type.134), calls=%async_computation.4 | async-start | bytes 131072 | tf_op jit(solution)/shard_map/all_to_all | solution.py:199
  1250.1 82.8 %all-to-all-start.3 = ((bf16[128,5,2048]{2,1,0:T(8,128)(2,1)}), bf16[128,5,2048]{2,1,0:T(8,128)(2,1)}, u32[]{:S(2)}, u32[]{:S(2)}) async-start(bf16[128,5,2048]{2,1,0:T(8,128)(2,1)} %reshape.302), calls=%async_computation.3 | async-start | bytes 8388608 | tf_op jit(solution)/shard_map/all_to_all | solution.py:192
  1262.2 50.9 %collective-permute-start.5 = (bf16[128,1,128]{2,0,1:T(8,128)(2,1)}, bf16[128,1,128]{2,0,1:T(8,128)(2,1)S(1)}, u32[]{:S(2)}, u32[]{:S(2)}) collective-permute-start(bf16[128,1,128]{2,0,1:T(8,128)(2,1)} %fusion.43), channel_id=1, source_target_pairs={{0,2},{2,4},{4,6},{6,8},{8,10},{10,12},{12,14},{14,16},{16,18},{18... | collective-permute-start | bytes 98312 | tf_op jit(solution)/shard_map/ppermute | solution.py:12
  1265.4 48.2 %collective-permute-start.4 = (bf16[128,1,128]{2,0,1:T(8,128)(2,1)S(1)}, bf16[128,1,128]{2,0,1:T(8,128)(2,1)}, u32[]{:S(2)}, u32[]{:S(2)}) collective-permute-start(bf16[128,1,128]{2,0,1:T(8,128)(2,1)S(1)} %fusion.46), channel_id=1, source_target_pairs={{0,2},{2,4},{4,6},{6,8},{8,10},{10,12},{12,14},{14,16},{16,18},{18... | collective-permute-start | bytes 98312 | tf_op jit(solution)/shard_map/ppermute | solution.py:12
  (303 other events, 3759.5 us)
where the time goes:
time: 1370 us; the launch traced here: 1350 us
  waiting for transfers between devices  584 us (43%)
  matrix products  502 us (37%)
  local copies, waits for them, and re-layouts  173 us (13%)
  starting transfers between devices  62.5 us (5%)
  other arithmetic  26.3 us (2%)
    ppermute x254, waiting for transfers between devices, shifted(): return lax.ppermute(value, axis, pairs)  547 us
    dot_general x64, matrix products, tile_grads(): jnp.einsum('iqk,kd->qid', score_grad, keys_flat, preferred_element_type=j...  133 us
    dot_general x64, matrix products, tile_grads(): jnp.einsum('iqk,qid->kd', score_grad, queries, preferred_element_type=jnp...  115 us
    while x252, local copies, waits for them, and re-layouts  95.8 us
    dot_general x64, matrix products, tile_grads(): jnp.einsum('qid,kd->iqk', queries, keys_flat, preferred_element_type=jnp....  79.1 us
    dot_general x64, matrix products, tile_grads(): jnp.einsum('qid,kd->iqk', grads_out, values_flat, preferred_element_type=...  75.7 us
    dot_general x64, matrix products, tile_grads(): jnp.einsum('iqk,qid->kd', probs_low, grads_out, preferred_element_type=jn...  55.4 us
    all_to_all x1, waiting for transfers between devices, shards(): lax.all_to_all(send_rows.reshape(experts, capacity, model_width), ('ctx',...  37.4 us
  transfers between devices with their start and end apart: 259, of which 253 were waited for; matrix products, arithmetic and copies ran while one was open for 48% of the time, Pallas kernels for 0%

commit v1 on v0

v1 whole, which is shorter than its diff:
```python
import functools
import math

import jax
import jax.numpy as jnp
from jax import lax
from jax.experimental import pallas as pl
from jax.experimental.pallas import tpu as pltpu
from jax.sharding import PartitionSpec as P

MESH = pl.DeviceIdType.MESH
LOG2E = 1.4426950408889634
F32 = jnp.float32
BF16 = jnp.bfloat16
CAP = 5
TILES = 16
DEVS = 128
CHIPS = 32
HALF = 64


def any_partner(step, c, k):
    s = lax.rem(step * 53, DEVS)
    x = lax.rem(c // 16 + lax.rem(s, 4), 4)
    s = s // 4
    y = lax.rem(lax.rem(c // 4, 4) + lax.rem(s, 4), 4)
    s = s // 4
    zh = lax.rem(lax.rem(c // 2, 2) + lax.rem(s, 2), 2)
    s = s // 2
    kk = lax.rem(k + lax.rem(s, 2), 2)
    core = lax.rem(lax.rem(c, 2) + s // 2, 2)
    return ((x * 4 + y) * 2 + zh) * 2 + core, kk


def chip_partner(step, c):
    x = lax.rem(c // 16 + lax.rem(step, 4), 4)
    s = step // 4
    y = lax.rem(lax.rem(c // 4, 4) + lax.rem(s, 4), 4)
    zh = lax.rem(lax.rem(c // 2, 2) + s // 4, 2)
    return (x * 4 + y) * 2 + zh


def dot(a, b):
    return jnp.dot(a, b, preferred_element_type=F32)


def dot_nt(a, b):
    return lax.dot_general(a, b, (((1,), (1,)), ((), ())), preferred_element_type=F32)


def dot_tn(a, b):
    return lax.dot_general(a, b, (((0,), (0,)), ((), ())), preferred_element_type=F32)


def slot_row(block, r):
    return pl.multiple_of((block // 4) * (CAP * HALF) + r * HALF + lax.rem(block, 4) * 16, 16)


def pack_block(block, perm, flat, chunks):
    cat = jnp.concatenate(
        [
            jnp.concatenate(
                [flat[pl.ds(slot_row(block, r), 16), k * 128 : (k + 1) * 128] for k in range(TILES)],
                axis=0,
            )
            for r in range(CAP)
        ],
        axis=1,
    )
    out = dot(perm, cat).astype(BF16)
    for r in range(CAP):
        chunks[pl.ds(block * 16, 16), r] = out[:, r * 128 : (r + 1) * 128].reshape(16, TILES, 128)


def unpack_block(block, perm, chunks, flat):
    cat = jnp.concatenate(
        [chunks[pl.ds(block * 16, 16), r].reshape(256, 128) for r in range(CAP)], axis=1
    )
    out = dot(perm, cat).astype(BF16)
    for r in range(CAP):
        for k in range(TILES):
            flat[pl.ds(slot_row(block, r), 16), k * 128 : (k + 1) * 128] = out[
                k * 16 : (k + 1) * 16, r * 128 : (r + 1) * 128
            ]


def layer_kernel(
    q_ref,
    k_ref,
    v_ref,
    o_ref,
    g_ref,
    log_ref,
    order_ref,
    rows_ref,
    mgrad_ref,
    ids_ref,
    gate_ref,
    wg_hbm,
    wu_hbm,
    wd_hbm,
    dq_ref,
    dk_ref,
    dv_ref,
    drows_ref,
    dgates_ref,
    gg_hbm,
    gu_hbm,
    gd_hbm,
    kv_own,
    kvb,
    dkb,
    rsb,
    qb,
    gb,
    st,
    dqs,
    dqr,
    perm_ref,
    send_a,
    send_b,
    recv_a,
    recv_b,
    back,
    gt_send,
    gt_recv,
    xb,
    yb,
    slb,
    wg,
    wu,
    wd,
    act_g,
    act_u,
    gub,
    hb,
    out_a,
    out_b,
    out_d,
    w_sem,
    out_sem,
    kv_sem,
    q_sem,
    a_sem,
    b_sem,
    rs_sem,
    dq_sem,
    ret_sem,
    gt_sem,
):
    c = lax.axis_index("ctx")
    k = lax.axis_index("kv")
    me = c * 2 + k
    chip = c // 2
    core = lax.rem(c, 2)
    other = chip * 2 + 1 - core
    score_scale = 1.0 / math.sqrt(128.0)

    weights = [
        pltpu.make_async_copy(src, dst, w_sem.at[i])
        for i, (src, dst) in enumerate(((wg_hbm, wg), (wu_hbm, wu), (wd_hbm, wd)))
    ]
    for copy in weights:
        copy.start()

    barrier = pltpu.get_barrier_semaphore()

    def greet(step, carry):
        pc, pk = any_partner(step, c, k)
        pl.semaphore_signal(barrier, inc=1, device_id=(pc, pk), device_id_type=MESH)
        return carry

    lax.fori_loop(1, DEVS, greet, 0)

    for h in range(2):
        kv_own[h, :, 0:128] = k_ref[h * HALF : (h + 1) * HALF, :]
        kv_own[h, :, 128:256] = v_ref[h * HALF : (h + 1) * HALF, :]
    qb[0] = q_ref[...]
    gb[0] = g_ref[...]
    prod = g_ref[...].astype(F32) * o_ref[...].astype(F32)
    hi = prod.astype(BF16)
    mid = (prod - hi.astype(F32)).astype(BF16)
    ones = jnp.ones((8, 128), BF16)
    delta = dot_nt(ones, hi) + dot_nt(ones, mid)
    row8 = lax.broadcasted_iota(jnp.int32, (8, 1024), 0)
    st[0] = jnp.where(row8 == 0, log_ref[...] * LOG2E, delta)

    lane = lax.broadcasted_iota(jnp.int32, (HALF, DEVS), 1)
    ids = ids_ref[...]
    gates = gate_ref[...].astype(F32)
    hits = [(ids[:, j : j + 1] == lane).astype(F32) for j in range(8)]
    named = functools.reduce(jnp.add, hits)
    gate_of = functools.reduce(jnp.add, [hits[j] * gates[:, j : j + 1] for j in range(8)])
    below = (
        lax.broadcasted_iota(jnp.int32, (HALF, HALF), 0)
        > lax.broadcasted_iota(jnp.int32, (HALF, HALF), 1)
    ).astype(BF16)
    rank = dot(below, named.astype(BF16))
    picks = [jnp.where(rank == float(r), named, 0.0) for r in range(CAP)]
    ri = lax.broadcasted_iota(jnp.int32, (256, 256), 0)
    ci = lax.broadcasted_iota(jnp.int32, (256, 256), 1)
    perm_ref[...] = (
        jnp.where(ri // 16 == lax.rem(ci, 16), 1.0, 0.0)
        * jnp.where(lax.rem(ri, 16) == ci // 16, 1.0, 0.0)
    ).astype(BF16)

    pl.semaphore_wait(barrier, DEVS - 1)

    def send_kv(step, carry):
        chip_to = chip_partner(step, c)
        pltpu.make_async_remote_copy(
            src_ref=kv_own,
            dst_ref=kvb.at[chip],
            send_sem=kv_sem.at[0],
            recv_sem=kv_sem.at[1],
            device_id=(chip_to * 2 + core, k),
            device_id_type=MESH,
        ).start()
        return carry

    to_core = [
        pltpu.make_async_remote_copy(
            src_ref=buf.at[0],
            dst_ref=buf.at[1],
            send_sem=q_sem.at[i],
            recv_sem=q_sem.at[3 + i],
            device_id=(other, k),
            device_id_type=MESH,
        )
        for i, buf in enumerate((qb, gb, st))
    ]
    for copy in to_core:
        copy.start()
    lax.fori_loop(1, CHIPS, send_kv, 0)
    kvb[pl.ds(chip, 1)] = kv_own[...].reshape(1, 2, HALF, 256)

    def dispatch(values, tables, flat, chunks, got, sems):
        for r in range(CAP):
            table = tables[r].astype(BF16)
            for n in range(4):
                part = dot_tn(table, values[:, n * 512 : (n + 1) * 512]).astype(BF16)
                for h in range(2):
                    flat[h * 320 + r * 64 : h * 320 + r * 64 + 64, n * 512 : (n + 1) * 512] = part[
                        h * 64 : (h + 1) * 64
                    ]

        def pack(block, carry):
            pack_block(block, perm_ref[...], flat, chunks)
            return carry

        lax.fori_loop(0, 8, pack, 0)

        send_all(chunks, got, sems)
        got[pl.ds(me, 1)] = chunks[pl.ds(me, 1)]

    def send_all(chunks, got, sems):
        def send(step, carry):
            pc, pk = any_partner(step, c, k)
            pltpu.make_async_remote_copy(
                src_ref=chunks.at[pc * 2 + pk],
                dst_ref=got.at[me],
                send_sem=sems.at[0],
                recv_sem=sems.at[1],
                device_id=(pc, pk),
                device_id_type=MESH,
            ).start()
            return carry

        lax.fori_loop(1, DEVS, send, 0)

    def wait_all(buf, sem, count):
        part = buf.at[pl.ds(0, count)]
        pltpu.make_async_copy(part, part, sem).wait()

    dispatch(rows_ref, picks, xb, send_a, recv_a, a_sem)
    dispatch(
        mgrad_ref,
        [jnp.where(p > 0.0, gate_of, 0.0) for p in picks],
        yb,
        send_b,
        recv_b,
        b_sem,
    )

    for copy in to_core:
        copy.wait()
    wait_all(kvb, kv_sem.at[0], CHIPS - 1)
    wait_all(kvb, kv_sem.at[1], CHIPS - 1)
    gap = (
        lax.broadcasted_iota(jnp.int32, (HALF, 512), 0)
        - lax.broadcasted_iota(jnp.int32, (HALF, 512), 1) // 8
    )
    dqs[...] = jnp.zeros_like(dqs)

    def key_tile(i, carry):
        for late_key in range(2):
            kv = kvb[pl.ds(i * 4, 4), late_key].reshape(256, 256)
            key_part = kv[:, 0:128]
            value_part = kv[:, 128:256]
            dk_sum = jnp.zeros((256, 128), F32)
            dv_sum = jnp.zeros((256, 128), F32)
            for late_q in range(late_key, 2):
                for who in range(2):
                    span = slice(late_q * 512, (late_q + 1) * 512)
                    qs = qb[who, span, :]
                    gs = gb[who, span, :]
                    shifted = dot_nt(key_part, qs) * (score_scale * LOG2E) - st[who, 0:1, span]
                    if late_q == late_key:
                        owner = c if who == 0 else other
                        own_stretch = order_ref[2 * owner + late_q]
                        pieces = []
                        for s in range(4):
                            key_stretch = order_ref[2 * ((i * 4 + s) * 2 + core) + late_key]
                            room = (own_stretch - key_stretch) * HALF
                            pieces.append(
                                jnp.where(gap <= room, shifted[s * HALF : (s + 1) * HALF], -1e30)
                            )
                        shifted = jnp.concatenate(pieces, axis=0)
                    probs = jnp.exp2(shifted)
                    dv_sum = dv_sum + dot(probs.astype(BF16), gs)
                    d_scores = (probs * (dot_nt(value_part, gs) - st[who, 1:2, span])).astype(BF16)
                    dk_sum = dk_sum + dot(d_scores, qs)
                    dqs[who, :, span] += dot_tn(key_part, d_scores)
            both = jnp.concatenate([dk_sum * score_scale, dv_sum], axis=1).astype(BF16)
            dkb[pl.ds(i * 4, 4), late_key] = both.reshape(4, HALF, 256)
        return carry

    lax.fori_loop(0, CHIPS // 4, key_tile, 0)

    dq_copy = pltpu.make_async_remote_copy(
        src_ref=dqs.at[1],
        dst_ref=dqr,
        send_sem=dq_sem.at[0],
        recv_sem=dq_sem.at[1],
        device_id=(other, k),
        device_id_type=MESH,
    )
    dq_copy.start()

    def send_partial(step, carry):
        chip_to = chip_partner(step, c)
        pltpu.make_async_remote_copy(
            src_ref=dkb.at[chip_to],
            dst_ref=rsb.at[chip],
            send_sem=rs_sem.at[0],
            recv_sem=rs_sem.at[1],
            device_id=(chip_to * 2 + core, k),
            device_id_type=MESH,
        ).start()
        return carry

    lax.fori_loop(1, CHIPS, send_partial, 0)
    rsb[pl.ds(chip, 1)] = dkb[pl.ds(chip, 1)]

    def unpack(chunks, flat):
        def body(block, carry):
            unpack_block(block, perm_ref[...], chunks, flat)
            return carry

        lax.fori_loop(0, 8, body, 0)

    wait_all(recv_a, a_sem.at[1], DEVS - 1)
    unpack(recv_a, xb)
    weights[0].wait()
    weights[1].wait()

    def gate_up(n, carry):
        cols = pl.ds(pl.multiple_of(n * 256, 256), 256)
        act_g[:, cols] = dot(xb[...], wg[:, cols])
        act_u[:, cols] = dot(xb[...], wu[:, cols])
        return carry

    lax.fori_loop(0, 3, gate_up, 0)
    weights[2].wait()
    wait_all(send_a, a_sem.at[0], DEVS - 1)
    wait_all(recv_b, b_sem.at[1], DEVS - 1)
    unpack(recv_b, yb)

    def hidden_part(n, gate_sum):
        cols = pl.ds(pl.multiple_of(n * 256, 256), 256)
        cols_up = pl.ds(pl.multiple_of(n * 256 + 768, 256), 256)
        projected = dot_nt(yb[...], wd[cols, :])
        ga = act_g[:, cols]
        ua = act_u[:, cols]
        sig = jax.nn.sigmoid(ga)
        silu = ga * sig
        hidden = (silu * ua).astype(BF16)
        hb[:, cols] = hidden
        gub[:, cols] = (projected * ua * sig * (1.0 + ga * (1.0 - sig))).astype(BF16)
        gub[:, cols_up] = (projected * silu).astype(BF16)
        return gate_sum + jnp.sum(projected * hidden.astype(F32), axis=1, keepdims=True)

    gate_sum = lax.fori_loop(0, 3, hidden_part, jnp.zeros((640, 1), F32))
    lane_h = lax.broadcasted_iota(jnp.int32, (HALF, 128), 1)
    for h in range(2):
        tile = jnp.zeros((HALF, 128), F32)
        for r in range(CAP):
            first = h * 320 + r * 64
            tile = jnp.where(lane_h == r, gate_sum[first : first + 64], tile)
        gt_send[h * HALF : (h + 1) * HALF] = jnp.broadcast_to(
            tile[:, None, :], (HALF, 16, 128)
        ).astype(BF16)
    send_all(gt_send, gt_recv, gt_sem)
    gt_recv[pl.ds(me, 1)] = gt_send[pl.ds(me, 1)]

    def slot_cols(n, carry):
        cols = pl.ds(pl.multiple_of(n * 256, 256), 256)
        slb[:, cols] = (
            dot_nt(gub[:, 0:768], wg[cols, :]) + dot_nt(gub[:, 768:1536], wu[cols, :])
        ).astype(BF16)
        return carry

    lax.fori_loop(0, 8, slot_cols, 0)

    def pack_back(block, carry):
        pack_block(block, perm_ref[...], slb, send_a)
        return carry

    lax.fori_loop(0, 8, pack_back, 0)
    send_all(send_a, back, ret_sem)
    back[pl.ds(me, 1)] = send_a[pl.ds(me, 1)]

    def grad_in(n, carry):
        rows = pl.ds(pl.multiple_of(n * 256, 256), 256)
        out_a[rows, :] = dot_tn(xb[:, rows], gub[:, 0:768]).astype(BF16)
        out_b[rows, :] = dot_tn(xb[:, rows], gub[:, 768:1536]).astype(BF16)
        return carry

    lax.fori_loop(0, 8, grad_in, 0)
    outs = [
        pltpu.make_async_copy(src, dst, out_sem.at[i])
        for i, (src, dst) in enumerate(((out_a, gg_hbm), (out_b, gu_hbm), (out_d, gd_hbm)))
    ]
    outs[0].start()
    outs[1].start()

    def grad_out(n, carry):
        cols = pl.ds(pl.multiple_of(n * 512, 512), 512)
        out_d[:, cols] = dot_tn(hb[...], yb[:, cols]).astype(BF16)
        return carry

    lax.fori_loop(0, 4, grad_out, 0)
    outs[2].start()

    wait_all(dkb, rs_sem.at[0], CHIPS - 1)
    wait_all(rsb, rs_sem.at[1], CHIPS - 1)

    def add_up(j, total):
        return total + rsb[j].astype(F32)

    total = lax.fori_loop(0, CHIPS, add_up, jnp.zeros((2, HALF, 256), F32))
    for h in range(2):
        dk_ref[h * HALF : (h + 1) * HALF, :] = total[h, :, 0:128].astype(BF16)
        dv_ref[h * HALF : (h + 1) * HALF, :] = total[h, :, 128:256].astype(BF16)
    dq_copy.wait()
    dq_ref[...] = jnp.transpose((dqs[0] + dqr[...]) * score_scale).astype(BF16)

    wait_all(gt_send, gt_sem.at[0], DEVS - 1)
    wait_all(gt_recv, gt_sem.at[1], DEVS - 1)
    slot_gates = jnp.transpose(gt_recv[...].astype(F32)[:, 0, :])
    gate_grads = functools.reduce(
        jnp.add, [picks[r] * slot_gates[r : r + 1, :] for r in range(CAP)]
    )
    lane8 = lax.broadcasted_iota(jnp.int32, (HALF, 8), 1)
    d_gates = jnp.zeros((HALF, 8), F32)
    for j in range(8):
        d_gates = jnp.where(
            lane8 == j, jnp.sum(hits[j] * gate_grads, axis=1, keepdims=True), d_gates
        )
    dgates_ref[...] = (d_gates / gates).astype(BF16)

    wait_all(send_b, b_sem.at[0], DEVS - 1)
    wait_all(send_a, ret_sem.at[0], DEVS - 1)
    wait_all(back, ret_sem.at[1], DEVS - 1)
    unpack(back, slb)
    tables = [picks[r].astype(BF16) for r in range(CAP)]

    def combine(n, carry):
        cols = pl.ds(pl.multiple_of(n * 512, 512), 512)
        acc = jnp.zeros((HALF, 512), F32)
        for r in range(CAP):
            for h in range(2):
                acc = acc + dot(
                    tables[r][:, h * 64 : (h + 1) * 64],
                    slb[h * 320 + r * 64 : h * 320 + r * 64 + 64, cols],
                )
        drows_ref[:, cols] = acc.astype(BF16)
        return carry

    lax.fori_loop(0, 4, combine, 0)
    for copy in outs:
        copy.wait()


def shards(
    query_rows,
    key_rows,
    value_rows,
    attn_out,
    attn_grad,
    log_total,
    stretch_order,
    moe_rows,
    moe_grad,
    expert_ids,
    gate_prob,
    gate_weight,
    up_weight,
    down_weight,
):
    tok, heads, size = query_rows.shape
    flat = tok * heads
    rows_here, width = moe_rows.shape
    hidden = gate_weight.shape[2]
    vmem = pl.BlockSpec(memory_space=pltpu.VMEM)
    smem = pl.BlockSpec(memory_space=pltpu.SMEM)
    hbm = pl.BlockSpec(memory_space=pl.ANY)
    chunk = (DEVS, CAP, TILES, 128)
    slots = DEVS * CAP
    results = pl.pallas_call(
        layer_kernel,
        out_shape=(
            jax.ShapeDtypeStruct((flat, size), BF16),
            jax.ShapeDtypeStruct((tok, size), BF16),
            jax.ShapeDtypeStruct((tok, size), BF16),
            jax.ShapeDtypeStruct((rows_here, width), BF16),
            jax.ShapeDtypeStruct((rows_here, 8), BF16),
            jax.ShapeDtypeStruct((width, hidden), BF16),
            jax.ShapeDtypeStruct((width, hidden), BF16),
            jax.ShapeDtypeStruct((hidden, width), BF16),
        ),
        in_specs=[vmem] * 6 + [smem] + [vmem] * 4 + [hbm] * 3,
        out_specs=(vmem,) * 5 + (hbm,) * 3,
        scratch_shapes=[
            pltpu.VMEM((2, HALF, 256), BF16),
            pltpu.VMEM((CHIPS, 2, HALF, 256), BF16),
            pltpu.VMEM((CHIPS, 2, HALF, 256), BF16),
            pltpu.VMEM((CHIPS, 2, HALF, 256), BF16),
            pltpu.VMEM((2, flat, size), BF16),
            pltpu.VMEM((2, flat, size), BF16),
            pltpu.VMEM((2, 8, flat), F32),
            pltpu.VMEM((2, size, flat), F32),
            pltpu.VMEM((size, flat), F32),
            pltpu.VMEM((256, 256), BF16),
            pltpu.VMEM(chunk, BF16),
            pltpu.VMEM(chunk, BF16),
            pltpu.VMEM(chunk, BF16),
            pltpu.VMEM(chunk, BF16),
            pltpu.VMEM(chunk, BF16),
            pltpu.VMEM((DEVS, 16, 128), BF16),
            pltpu.VMEM((DEVS, 16, 128), BF16),
            pltpu.VMEM((slots, width), BF16),
            pltpu.VMEM((slots, width), BF16),
            pltpu.VMEM((slots, width), BF16),
            pltpu.VMEM((width, hidden), BF16),
            pltpu.VMEM((width, hidden), BF16),
            pltpu.VMEM((hidden, width), BF16),
            pltpu.VMEM((slots, hidden), F32),
            pltpu.VMEM((slots, hidden), F32),
            pltpu.VMEM((slots, 2 * hidden), BF16),
            pltpu.VMEM((slots, hidden), BF16),
            pltpu.VMEM((width, hidden), BF16),
            pltpu.VMEM((width, hidden), BF16),
            pltpu.VMEM((hidden, width), BF16),
            pltpu.SemaphoreType.DMA((3,)),
            pltpu.SemaphoreType.DMA((3,)),
            pltpu.SemaphoreType.DMA((2,)),
            pltpu.SemaphoreType.DMA((6,)),
            pltpu.SemaphoreType.DMA((2,)),
            pltpu.SemaphoreType.DMA((2,)),
            pltpu.SemaphoreType.DMA((2,)),
            pltpu.SemaphoreType.DMA((2,)),
            pltpu.SemaphoreType.DMA((2,)),
            pltpu.SemaphoreType.DMA((2,)),
        ],
        compiler_params=pltpu.CompilerParams(
            collective_id=0, has_side_effects=True, vmem_limit_bytes=62 * 1024 * 1024
        ),
    )(
        query_rows.reshape(flat, size),
        key_rows.reshape(tok, size),
        value_rows.reshape(tok, size),
        attn_out.reshape(flat, size),
        attn_grad.reshape(flat, size),
        log_total.reshape(1, flat),
        stretch_order,
        moe_rows,
        moe_grad,
        expert_ids,
        gate_prob,
        gate_weight[0],
        up_weight[0],
        down_weight[0],
    )
    d_query, d_key, d_value, d_rows, d_gates, grad_gate, grad_up, grad_down = results
    return (
        d_query.reshape(tok, heads, size),
        d_key.reshape(tok, 1, size),
        d_value.reshape(tok, 1, size),
        d_rows,
        d_gates,
        grad_gate[None],
        grad_up[None],
        grad_down[None],
    )


def solution(mesh):
    both = ("ctx", "kv")
    heads = P("ctx", "kv", None)
    tokens = P(both, None)
    experts = P(both, None, None)
    return jax.shard_map(
        shards,
        mesh=mesh,
        in_specs=(heads,) * 5
        + (P("ctx", "kv"), P())
        + (tokens,) * 4
        + (experts,) * 3,
        out_specs=(heads,) * 3 + (tokens,) * 2 + (experts,) * 3,
        check_vma=False,
    )
```

time: 1370 us -> 204 us (0.15)
  the two profiles are of different devices: /device:TPU:0 before, /device:TPU:21 now
where the time goes in v1:
time: 204 us; the launch traced here: 202 us
  Pallas kernels  181 us (89%)
  local copies, waits for them, and re-layouts  20.3 us (10%)
    pallas_call x1, Pallas kernels, shards(): pl.pallas_call(layer_kernel, out_shape=(jax.ShapeDtypeStruct((flat, size)...  181 us
    unnamed x15, local copies, waits for them, and re-layouts  19.6 us

profile of v1, /device:TPU:21, one launch (start us, length us, event | category | flops | bytes accessed | tf_op | source)
XLA Modules:
  0.0 202.2 jit_solution(13741197222079920077)
XLA Ops:
  0.6 1.4 copy.28.gate_ref
  2.0 1.4 copy.27.ids_ref
  3.4 0.8 copy.26
  4.2 0.7 reshape.48.log_ref
  4.9 181.3 %shard_map.197 = (bf16[1024,128]{1,0:T(8,128)(2,1)}, bf16[128,128]{1,0:T(8,128)(2,1)}, bf16[128,128]{1,0:T(8,128)(2,1)}, bf16[64,2048]{1,0:T(8,128)(2,1)}, bf16[...) custom-call(bf16[1024,128]{1,0:T(8,128)(2,1)} %bitcast.20, ...), custom_call_target="tpu_custom_call" | custom-call | tf_op jit(solution)/shard_map/pallas_call | solution.py:520
  186.1 1.4 copy.29
  187.5 1.7 copy.37
  189.2 1.4 copy.38
  190.6 1.4 copy.39
  191.9 1.7 copy.40
  193.6 0.0 copy-start.1
  193.6 3.9 %copy.41 = bf16[1,2048,768]{2,1,0:T(8,128)(2,1)} copy(bf16[1,2048,768]{2,1,0:T(8,128)(2,1)} %bitcast.16) | data formatting | bytes 6291456
  197.5 0.0 copy-done.1
  197.5 0.0 copy-start
  197.5 1.7 copy.42
  199.2 1.4 copy-done
  200.5 1.7 copy.43
Async XLA Ops:
  193.6 3.9 %copy-start.1 = (bf16[2048,768]{1,0:T(8,128)(2,1)S(1)}, bf16[2048,768]{1,0:T(8,128)(2,1)}, u32[]{:S(2)}) copy-start(bf16[2048,768]{1,0:T(8,128)(2,1)} %get-tuple-element.22) | copy-start | bytes 9437188
  197.5 3.0 %copy-start = (bf16[768,2048]{1,0:T(8,128)(2,1)S(1)}, bf16[768,2048]{1,0:T(8,128)(2,1)}, u32[]{:S(2)}) copy-start(bf16[768,2048]{1,0:T(8,128)(2,1)} %get-tuple-element.23) | copy-start | bytes 9437188

commit v2 on v1

--- a/solution.py
+++ b/solution.py
@@ -19,25 +19,22 @@
 HALF = 64
 
 
-def any_partner(step, c, k):
-    s = lax.rem(step * 53, DEVS)
+def chip_step(step, c, k):
+    s = lax.rem(step * 29, 64)
     x = lax.rem(c // 16 + lax.rem(s, 4), 4)
     s = s // 4
     y = lax.rem(lax.rem(c // 4, 4) + lax.rem(s, 4), 4)
-    s = s // 4
-    zh = lax.rem(lax.rem(c // 2, 2) + lax.rem(s, 2), 2)
-    s = s // 2
-    kk = lax.rem(k + lax.rem(s, 2), 2)
-    core = lax.rem(lax.rem(c, 2) + s // 2, 2)
-    return ((x * 4 + y) * 2 + zh) * 2 + core, kk
-
-
-def chip_partner(step, c):
-    x = lax.rem(c // 16 + lax.rem(step, 4), 4)
-    s = step // 4
-    y = lax.rem(lax.rem(c // 4, 4) + lax.rem(s, 4), 4)
-    zh = lax.rem(lax.rem(c // 2, 2) + s // 4, 2)
-    return (x * 4 + y) * 2 + zh
+    z = lax.rem(lax.rem(c // 2, 2) * 2 + k + s // 4, 4)
+    return (x * 4 + y) * 2 + z // 2, lax.rem(z, 2)
+
+
+def any_partner(step, c, k):
+    chip, kk = chip_step(step // 2, c, k)
+    return chip * 2 + lax.rem(lax.rem(c, 2) + lax.rem(step, 2), 2), kk
+
+
+def place(c, k):
+    return lax.rem(c, 2) * 64 + (c // 2) * 2 + k
 
 
 def dot(a, b):
@@ -110,7 +107,11 @@
     kv_own,
     kvb,
     dkb,
-    rsb,
+    rs1,
+    mid,
+    rs2,
+    table,
+    gtable,
     qb,
     gb,
     st,
@@ -150,10 +151,17 @@
 ):
     c = lax.axis_index("ctx")
     k = lax.axis_index("kv")
-    me = c * 2 + k
+    me = place(c, k)
     chip = c // 2
     core = lax.rem(c, 2)
     other = chip * 2 + 1 - core
+    zh = lax.rem(chip, 2)
+    at_x = chip // 8
+    at_y = lax.rem(chip // 2, 4)
+    at_b = at_x * (1 - core) + at_y * core
+    at_m = at_y * (1 - core) + at_x * core
+    step_b = 8 - 6 * core
+    step_m = 2 + 6 * core
     score_scale = 1.0 / math.sqrt(128.0)
 
     weights = [
@@ -179,24 +187,46 @@
     gb[0] = g_ref[...]
     prod = g_ref[...].astype(F32) * o_ref[...].astype(F32)
     hi = prod.astype(BF16)
-    mid = (prod - hi.astype(F32)).astype(BF16)
+    low = (prod - hi.astype(F32)).astype(BF16)
     ones = jnp.ones((8, 128), BF16)
-    delta = dot_nt(ones, hi) + dot_nt(ones, mid)
+    delta = dot_nt(ones, hi) + dot_nt(ones, low)
+    logs = log_ref[...]
+    log_hi = logs.astype(BF16)
+    rest = logs - log_hi.astype(F32)
+    log_mid = rest.astype(BF16)
+    log_low = (rest - log_mid.astype(F32)).astype(BF16)
+    spread = (
+        lax.broadcasted_iota(jnp.int32, (128, 1024), 1) // 8
+        == lax.broadcasted_iota(jnp.int32, (128, 1024), 0)
+    ).astype(BF16)
+    wide = dot(log_hi, spread) + dot(log_mid, spread) + dot(log_low, spread)
     row8 = lax.broadcasted_iota(jnp.int32, (8, 1024), 0)
-    st[0] = jnp.where(row8 == 0, log_ref[...] * LOG2E, delta)
-
-    lane = lax.broadcasted_iota(jnp.int32, (HALF, DEVS), 1)
-    ids = ids_ref[...]
+    mine = row8 == lax.rem(lax.broadcasted_iota(jnp.int32, (8, 1024), 1), 8)
+    log_row = jnp.sum(jnp.where(mine, wide, 0.0), axis=0, keepdims=True)
+    st[0] = jnp.where(row8 == 0, log_row * LOG2E, delta)
+
+    spot = lax.broadcasted_iota(jnp.int32, (DEVS, HALF), 0)
+    expert = (lax.rem(spot, 64) // 2) * 4 + (spot // 64) * 2 + lax.rem(spot, 2)
     gates = gate_ref[...].astype(F32)
-    hits = [(ids[:, j : j + 1] == lane).astype(F32) for j in range(8)]
-    named = functools.reduce(jnp.add, hits)
-    gate_of = functools.reduce(jnp.add, [hits[j] * gates[:, j : j + 1] for j in range(8)])
-    below = (
+
+    def hit(j):
+        return jnp.where(expert == ids_ref[j : j + 1, :], 1.0, 0.0)
+
+    named = functools.reduce(jnp.add, [hit(j) for j in range(8)])
+    gate_of = functools.reduce(jnp.add, [hit(j) * gates[j : j + 1, :] for j in range(8)])
+    before = (
         lax.broadcasted_iota(jnp.int32, (HALF, HALF), 0)
-        > lax.broadcasted_iota(jnp.int32, (HALF, HALF), 1)
+        < lax.broadcasted_iota(jnp.int32, (HALF, HALF), 1)
     ).astype(BF16)
-    rank = dot(below, named.astype(BF16))
-    picks = [jnp.where(rank == float(r), named, 0.0) for r in range(CAP)]
+    rank = dot(named.astype(BF16), before)
+    for r in range(CAP):
+        pick = jnp.where(rank == float(r), named, 0.0)
+        scaled = (pick * gate_of).astype(BF16)
+        pick = pick.astype(BF16)
+        for h in range(2):
+            first = h * 320 + r * 64
+            table[first : first + 64, :] = pick[h * 64 : (h + 1) * 64]
+            gtable[first : first + 64, :] = scaled[h * 64 : (h + 1) * 64]
     ri = lax.broadcasted_iota(jnp.int32, (256, 256), 0)
     ci = lax.broadcasted_iota(jnp.int32, (256, 256), 1)
     perm_ref[...] = (
@@ -204,19 +234,45 @@
         * jnp.where(lax.rem(ri, 16) == ci // 16, 1.0, 0.0)
     ).astype(BF16)
 
-    pl.semaphore_wait(barrier, DEVS - 1)
-
-    def send_kv(step, carry):
-        chip_to = chip_partner(step, c)
+    def gather(values, chosen, flat, chunks):
+        def cols(n, carry):
+            span = pl.ds(pl.multiple_of(n * 512, 512), 512)
+            flat[:, span] = dot(chosen[...], values[:, span]).astype(BF16)
+            return carry
+
+        lax.fori_loop(0, 4, cols, 0)
+
+        def pack(block, carry):
+            pack_block(block, perm_ref[...], flat, chunks)
+            return carry
+
+        lax.fori_loop(0, 8, pack, 0)
+
+    def send_to(pc, pk, chunks, got, sems):
         pltpu.make_async_remote_copy(
-            src_ref=kv_own,
-            dst_ref=kvb.at[chip],
-            send_sem=kv_sem.at[0],
-            recv_sem=kv_sem.at[1],
-            device_id=(chip_to * 2 + core, k),
+            src_ref=chunks.at[place(pc, pk)],
+            dst_ref=got.at[me],
+            send_sem=sems.at[0],
+            recv_sem=sems.at[1],
+            device_id=(pc, pk),
             device_id_type=MESH,
         ).start()
-        return carry
+
+    def send_all(chunks, got, sems):
+        def send(step, carry):
+            pc, pk = any_partner(step, c, k)
+            send_to(pc, pk, chunks, got, sems)
+            return carry
+
+        lax.fori_loop(1, DEVS, send, 0)
+
+    def wait_all(buf, sem, count):
+        part = buf.at[pl.ds(0, count)]
+        pltpu.make_async_copy(part, part, sem).wait()
+
+    gather(rows_ref, table, xb, send_a)
+
+    pl.semaphore_wait(barrier, DEVS - 1)
 
     to_core = [
         pltpu.make_async_remote_copy(
@@ -231,61 +287,53 @@
     ]
     for copy in to_core:
         copy.start()
-    lax.fori_loop(1, CHIPS, send_kv, 0)
+
+    def near(step):
+        return lax.rem(at_m + lax.rem(step, 4), 4), lax.rem(zh + step // 4, 2)
+
+    def send_kv(step, carry):
+        m, z = near(step)
+        pltpu.make_async_remote_copy(
+            src_ref=kv_own,
+            dst_ref=kvb.at[chip],
+            send_sem=kv_sem.at[0],
+            recv_sem=kv_sem.at[1],
+            device_id=((at_b * step_b + m * step_m + z) * 2 + core, k),
+            device_id_type=MESH,
+        ).start()
+        return carry
+
+    lax.fori_loop(1, 8, send_kv, 0)
+    send_all(send_a, recv_a, a_sem)
+    recv_a[pl.ds(me, 1)] = send_a[pl.ds(me, 1)]
     kvb[pl.ds(chip, 1)] = kv_own[...].reshape(1, 2, HALF, 256)
-
-    def dispatch(values, tables, flat, chunks, got, sems):
-        for r in range(CAP):
-            table = tables[r].astype(BF16)
-            for n in range(4):
-                part = dot_tn(table, values[:, n * 512 : (n + 1) * 512]).astype(BF16)
-                for h in range(2):
-                    flat[h * 320 + r * 64 : h * 320 + r * 64 + 64, n * 512 : (n + 1) * 512] = part[
-                        h * 64 : (h + 1) * 64
-                    ]
-
-        def pack(block, carry):
-            pack_block(block, perm_ref[...], flat, chunks)
-            return carry
-
-        lax.fori_loop(0, 8, pack, 0)
-
-        send_all(chunks, got, sems)
-        got[pl.ds(me, 1)] = chunks[pl.ds(me, 1)]
-
-    def send_all(chunks, got, sems):
-        def send(step, carry):
-            pc, pk = any_partner(step, c, k)
-            pltpu.make_async_remote_copy(
-                src_ref=chunks.at[pc * 2 + pk],
-                dst_ref=got.at[me],
-                send_sem=sems.at[0],
-                recv_sem=sems.at[1],
-                device_id=(pc, pk),
-                device_id_type=MESH,
-            ).start()
-            return carry
-
-        lax.fori_loop(1, DEVS, send, 0)
-
-    def wait_all(buf, sem, count):
-        part = buf.at[pl.ds(0, count)]
-        pltpu.make_async_copy(part, part, sem).wait()
-
-    dispatch(rows_ref, picks, xb, send_a, recv_a, a_sem)
-    dispatch(
-        mgrad_ref,
-        [jnp.where(p > 0.0, gate_of, 0.0) for p in picks],
-        yb,
-        send_b,
-        recv_b,
-        b_sem,
-    )
+    wait_all(kvb, kv_sem.at[1], 7)
+
+    def pass_kv(step, carry):
+        b = lax.rem(at_b + 1 + lax.rem(step, 3), 4)
+        i = step // 3
+        block = at_b * step_b + (i // 2) * step_m + lax.rem(i, 2)
+        pltpu.make_async_remote_copy(
+            src_ref=kvb.at[block],
+            dst_ref=kvb.at[block],
+            send_sem=kv_sem.at[2],
+            recv_sem=kv_sem.at[3],
+            device_id=((b * step_b + at_m * step_m + zh) * 2 + core, k),
+            device_id_type=MESH,
+        ).start()
+        return carry
+
+    lax.fori_loop(0, 24, pass_kv, 0)
+
+    gather(mgrad_ref, gtable, yb, send_b)
+    send_all(send_b, recv_b, b_sem)
+    recv_b[pl.ds(me, 1)] = send_b[pl.ds(me, 1)]
 
     for copy in to_core:
         copy.wait()
-    wait_all(kvb, kv_sem.at[0], CHIPS - 1)
-    wait_all(kvb, kv_sem.at[1], CHIPS - 1)
+    wait_all(kvb, kv_sem.at[0], 7)
+    wait_all(kvb, kv_sem.at[2], 24)
+    wait_all(kvb, kv_sem.at[3], 24)
     gap = (
         lax.broadcasted_iota(jnp.int32, (HALF, 512), 0)
         - lax.broadcasted_iota(jnp.int32, (HALF, 512), 1) // 8
@@ -338,19 +386,30 @@
     dq_copy.start()
 
     def send_partial(step, carry):
-        chip_to = chip_partner(step, c)
+        shift = 1 + lax.rem(step, 3)
+        b = lax.rem(at_b + shift, 4)
+        i = step // 3
         pltpu.make_async_remote_copy(
-            src_ref=dkb.at[chip_to],
-            dst_ref=rsb.at[chip],
+            src_ref=dkb.at[b * step_b + (i // 2) * step_m + lax.rem(i, 2)],
+            dst_ref=rs1.at[(shift - 1) * 8 + i],
             send_sem=rs_sem.at[0],
             recv_sem=rs_sem.at[1],
-            device_id=(chip_to * 2 + core, k),
+            device_id=((b * step_b + at_m * step_m + zh) * 2 + core, k),
             device_id_type=MESH,
         ).start()
         return carry
 
-    lax.fori_loop(1, CHIPS, send_partial, 0)
-    rsb[pl.ds(chip, 1)] = dkb[pl.ds(chip, 1)]
+    def send_mid(step, carry):
+        m, z = near(step)
+        pltpu.make_async_remote_copy(
+            src_ref=mid.at[m * 2 + z],
+            dst_ref=rs2.at[step - 1],
+            send_sem=rs_sem.at[2],
+            recv_sem=rs_sem.at[3],
+            device_id=((at_b * step_b + m * step_m + z) * 2 + core, k),
+            device_id_type=MESH,
+        ).start()
+        return carry
 
     def unpack(chunks, flat):
         def body(block, carry):
@@ -374,6 +433,7 @@
     weights[2].wait()
     wait_all(send_a, a_sem.at[0], DEVS - 1)
     wait_all(recv_b, b_sem.at[1], DEVS - 1)
+    lax.fori_loop(0, 24, send_partial, 0)
     unpack(recv_b, yb)
 
     def hidden_part(n, gate_sum):
@@ -403,22 +463,47 @@
     send_all(gt_send, gt_recv, gt_sem)
     gt_recv[pl.ds(me, 1)] = gt_send[pl.ds(me, 1)]
 
-    def slot_cols(n, carry):
-        cols = pl.ds(pl.multiple_of(n * 256, 256), 256)
-        slb[:, cols] = (
-            dot_nt(gub[:, 0:768], wg[cols, :]) + dot_nt(gub[:, 768:1536], wu[cols, :])
-        ).astype(BF16)
-        return carry
-
-    lax.fori_loop(0, 8, slot_cols, 0)
-
-    def pack_back(block, carry):
-        pack_block(block, perm_ref[...], slb, send_a)
-        return carry
-
-    lax.fori_loop(0, 8, pack_back, 0)
-    send_all(send_a, back, ret_sem)
+    for h in range(2):
+        span = slice(h * 320, (h + 1) * 320)
+
+        def slot_cols(n, carry):
+            cols = pl.ds(pl.multiple_of(n * 256, 256), 256)
+            slb[span, cols] = (
+                dot_nt(gub[span, 0:768], wg[cols, :]) + dot_nt(gub[span, 768:1536], wu[cols, :])
+            ).astype(BF16)
+            return carry
+
+        lax.fori_loop(0, 8, slot_cols, 0)
+
+        def pack_back(block, carry):
+            pack_block(block, perm_ref[...], slb, send_a)
+            return carry
+
+        lax.fori_loop(h * 4, h * 4 + 4, pack_back, 0)
+
+        @pl.when(core != h)
+        def _():
+            send_to(chip * 2 + h, k, send_a, back, ret_sem)
+
+        def send_half(step, carry):
+            pc, pk = chip_step(step, c, k)
+            send_to(pc * 2 + h, pk, send_a, back, ret_sem)
+            return carry
+
+        lax.fori_loop(1, 64, send_half, 0)
     back[pl.ds(me, 1)] = send_a[pl.ds(me, 1)]
+
+    wait_all(rs1, rs_sem.at[1], 24)
+
+    def line_sum(i, carry):
+        own = dkb[at_b * step_b + (i // 2) * step_m + lax.rem(i, 2)].astype(F32)
+        for s in range(3):
+            own = own + rs1[s * 8 + i].astype(F32)
+        mid[i] = own.astype(BF16)
+        return carry
+
+    lax.fori_loop(0, 8, line_sum, 0)
+    lax.fori_loop(1, 8, send_mid, 0)
 
     def grad_in(n, carry):
         rows = pl.ds(pl.multiple_of(n * 256, 256), 256)
@@ -442,13 +527,12 @@
     lax.fori_loop(0, 4, grad_out, 0)
     outs[2].start()
 
-    wait_all(dkb, rs_sem.at[0], CHIPS - 1)
-    wait_all(rsb, rs_sem.at[1], CHIPS - 1)
-
-    def add_up(j, total):
-        return total + rsb[j].astype(F32)
-
-    total = lax.fori_loop(0, CHIPS, add_up, jnp.zeros((2, HALF, 256), F32))
+    wait_all(rs1, rs_sem.at[0], 24)
+    wait_all(rs2, rs_sem.at[2], 7)
+    wait_all(rs2, rs_sem.at[3], 7)
+    total = mid[at_m * 2 + zh].astype(F32)
+    for s in range(7):
+        total = total + rs2[s].astype(F32)
     for h in range(2):
         dk_ref[h * HALF : (h + 1) * HALF, :] = total[h, :, 0:128].astype(BF16)
         dv_ref[h * HALF : (h + 1) * HALF, :] = total[h, :, 128:256].astype(BF16)
@@ -457,39 +541,63 @@
 
     wait_all(gt_send, gt_sem.at[0], DEVS - 1)
     wait_all(gt_recv, gt_sem.at[1], DEVS - 1)
-    slot_gates = jnp.transpose(gt_recv[...].astype(F32)[:, 0, :])
-    gate_grads = functools.reduce(
-        jnp.add, [picks[r] * slot_gates[r : r + 1, :] for r in range(CAP)]
-    )
-    lane8 = lax.broadcasted_iota(jnp.int32, (HALF, 8), 1)
-    d_gates = jnp.zeros((HALF, 8), F32)
+    slot_gates = gt_recv[...].astype(F32)[:, 0, :]
+    halves = []
+    for h in range(2):
+        acc = jnp.zeros((64, HALF), F32)
+        for r in range(CAP):
+            first = h * 320 + r * 64
+            acc = acc + table[first : first + 64, :].astype(F32) * slot_gates[
+                h * 64 : (h + 1) * 64, r : r + 1
+            ]
+        halves.append(acc)
+    gate_grads = jnp.concatenate(halves, axis=0)
     for j in range(8):
-        d_gates = jnp.where(
-            lane8 == j, jnp.sum(hits[j] * gate_grads, axis=1, keepdims=True), d_gates
-        )
-    dgates_ref[...] = (d_gates / gates).astype(BF16)
+        dgates_ref[j : j + 1, :] = (
+            jnp.sum(hit(j) * gate_grads, axis=0, keepdims=True) / gates[j : j + 1, :]
+        ).astype(BF16)
 
     wait_all(send_b, b_sem.at[0], DEVS - 1)
     wait_all(send_a, ret_sem.at[0], DEVS - 1)
     wait_all(back, ret_sem.at[1], DEVS - 1)
     unpack(back, slb)
-    tables = [picks[r].astype(BF16) for r in range(CAP)]
 
     def combine(n, carry):
         cols = pl.ds(pl.multiple_of(n * 512, 512), 512)
-        acc = jnp.zeros((HALF, 512), F32)
-        for r in range(CAP):
-            for h in range(2):
-                acc = acc + dot(
-                    tables[r][:, h * 64 : (h + 1) * 64],
-                    slb[h * 320 + r * 64 : h * 320 + r * 64 + 64, cols],
-                )
-        drows_ref[:, cols] = acc.astype(BF16)
+        drows_ref[:, cols] = dot_tn(table[...], slb[:, cols]).astype(BF16)
         return carry
 
     lax.fori_loop(0, 4, combine, 0)
     for copy in outs:
         copy.wait()
+
+
+def hand_over(*refs):
+    small, big = refs[0:5], refs[5:8]
+    small_out, big_out = refs[8:13], refs[13:16]
+    held, in_sem, out_sem = refs[16:19], refs[19], refs[20]
+    steps = []
+    for i in range(3):
+        count = 4
+        depth = big[i].shape[0] // count
+        for part in range(count):
+            rows = pl.ds(part * depth, depth)
+            sem = i * count + part
+            steps.append(
+                (
+                    pltpu.make_async_copy(big[i].at[rows], held[i].at[rows], in_sem.at[sem]),
+                    pltpu.make_async_copy(held[i].at[rows], big_out[i].at[rows], out_sem.at[sem]),
+                )
+            )
+    for fetch, _ in steps:
+        fetch.start()
+    for src, dst in zip(small, small_out):
+        dst[...] = src[...]
+    for fetch, store in steps:
+        fetch.wait()
+        store.start()
+    for _, store in steps:
+        store.wait()
 
 
 def shards(
@@ -517,25 +625,30 @@
     hbm = pl.BlockSpec(memory_space=pl.ANY)
     chunk = (DEVS, CAP, TILES, 128)
     slots = DEVS * CAP
+    shapes = (
+        jax.ShapeDtypeStruct((flat, size), BF16),
+        jax.ShapeDtypeStruct((tok, size), BF16),
+        jax.ShapeDtypeStruct((tok, size), BF16),
+        jax.ShapeDtypeStruct((rows_here, width), BF16),
+        jax.ShapeDtypeStruct((8, rows_here), BF16),
+        jax.ShapeDtypeStruct((width, hidden), BF16),
+        jax.ShapeDtypeStruct((width, hidden), BF16),
+        jax.ShapeDtypeStruct((hidden, width), BF16),
+    )
     results = pl.pallas_call(
         layer_kernel,
-        out_shape=(
-            jax.ShapeDtypeStruct((flat, size), BF16),
-            jax.ShapeDtypeStruct((tok, size), BF16),
-            jax.ShapeDtypeStruct((tok, size), BF16),
-            jax.ShapeDtypeStruct((rows_here, width), BF16),
-            jax.ShapeDtypeStruct((rows_here, 8), BF16),
-            jax.ShapeDtypeStruct((width, hidden), BF16),
-            jax.ShapeDtypeStruct((width, hidden), BF16),
-            jax.ShapeDtypeStruct((hidden, width), BF16),
-        ),
+        out_shape=shapes,
         in_specs=[vmem] * 6 + [smem] + [vmem] * 4 + [hbm] * 3,
         out_specs=(vmem,) * 5 + (hbm,) * 3,
         scratch_shapes=[
             pltpu.VMEM((2, HALF, 256), BF16),
             pltpu.VMEM((CHIPS, 2, HALF, 256), BF16),
             pltpu.VMEM((CHIPS, 2, HALF, 256), BF16),
-            pltpu.VMEM((CHIPS, 2, HALF, 256), BF16),
+            pltpu.VMEM((24, 2, HALF, 256), BF16),
+            pltpu.VMEM((8, 2, HALF, 256), BF16),
+            pltpu.VMEM((7, 2, HALF, 256), BF16),
+            pltpu.VMEM((slots, HALF), BF16),
+            pltpu.VMEM((slots, HALF), BF16),
             pltpu.VMEM((2, flat, size), BF16),
             pltpu.VMEM((2, flat, size), BF16),
             pltpu.VMEM((2, 8, flat), F32),
@@ -564,11 +677,11 @@
             pltpu.VMEM((hidden, width), BF16),
             pltpu.SemaphoreType.DMA((3,)),
             pltpu.SemaphoreType.DMA((3,)),
-            pltpu.SemaphoreType.DMA((2,)),
+            pltpu.SemaphoreType.DMA((4,)),
             pltpu.SemaphoreType.DMA((6,)),
             pltpu.SemaphoreType.DMA((2,)),
             pltpu.SemaphoreType.DMA((2,)),
-            pltpu.SemaphoreType.DMA((2,)),
+            pltpu.SemaphoreType.DMA((4,)),
             pltpu.SemaphoreType.DMA((2,)),
             pltpu.SemaphoreType.DMA((2,)),
             pltpu.SemaphoreType.DMA((2,)),
@@ -582,23 +695,32 @@
         value_rows.reshape(tok, size),
         attn_out.reshape(flat, size),
         attn_grad.reshape(flat, size),
-        log_total.reshape(1, flat),
+        log_total.T,
         stretch_order,
         moe_rows,
         moe_grad,
-        expert_ids,
-        gate_prob,
+        expert_ids.T,
+        gate_prob.T,
         gate_weight[0],
         up_weight[0],
         down_weight[0],
     )
+    results = pl.pallas_call(
+        hand_over,
+        out_shape=shapes,
+        in_specs=[vmem] * 5 + [hbm] * 3,
+        out_specs=(vmem,) * 5 + (hbm,) * 3,
+        scratch_shapes=[pltpu.VMEM(shape.shape, BF16) for shape in shapes[5:8]]
+        + [pltpu.SemaphoreType.DMA((12,))] * 2,
+        compiler_params=pltpu.CompilerParams(vmem_limit_bytes=60 * 1024 * 1024),
+    )(*results)
     d_query, d_key, d_value, d_rows, d_gates, grad_gate, grad_up, grad_down = results
     return (
         d_query.reshape(tok, heads, size),
         d_key.reshape(tok, 1, size),
         d_value.reshape(tok, 1, size),
         d_rows,
-        d_gates,
+        d_gates.T,
         grad_gate[None],
         grad_up[None],
         grad_down[None],

time: 204 us -> 186 us (0.912)
  local copies, waits for them, and re-layouts: 20.3 us -> 0 us
    unnamed x15 -> x0, local copies, waits for them, and re-layouts: 19.6 us -> none
    pallas_call x1 -> x2, Pallas kernels: 181 us -> 182 us  [the longest x1 173 us: shards(): pl.pallas_call(layer_kernel, out_shape=shapes, in_specs=[vmem] * 6 + [sme...]
where the time goes in v2:
time: 186 us; the launch traced here: 183 us
  Pallas kernels  182 us (98%)
    pallas_call x1, Pallas kernels, shards(): pl.pallas_call(layer_kernel, out_shape=shapes, in_specs=[vmem] * 6 + [sme...  173 us
    pallas_call x1, Pallas kernels, shards(): pl.pallas_call(hand_over, out_shape=shapes, in_specs=[vmem] * 5 + [hbm] *...  9.13 us

profile of v2, /device:TPU:21, one launch (start us, length us, event | category | flops | bytes accessed | tf_op | source)
XLA Modules:
  0.0 182.9 jit_solution(12539470323382335035)
XLA Ops:
  0.6 173.1 %shard_map.197 = (bf16[1024,128]{1,0:T(8,128)(2,1)}, bf16[128,128]{1,0:T(8,128)(2,1)}, bf16[128,128]{1,0:T(8,128)(2,1)}, bf16[64,2048]{1,0:T(8,128)(2,1)}, bf16[...) custom-call(bf16[1024,128]{1,0:T(8,128)(2,1)} %bitcast.21, ...), custom_call_target="tpu_custom_call" | custom-call | tf_op jit(solution)/shard_map/pallas_call | solution.py:638
  173.8 9.1 %shard_map.198 = (bf16[1024,128]{1,0:T(8,128)(2,1)}, bf16[128,128]{1,0:T(8,128)(2,1)}, bf16[128,128]{1,0:T(8,128)(2,1)}, bf16[64,2048]{1,0:T(8,128)(2,1)}, bf16[...) custom-call(bf16[1024,128]{1,0:T(8,128)(2,1)} %get-tuple-element.24.refs_0_, ...), custom_call_target="tpu_custom_call" | custom-call | tf_op jit(solution)/shard_map/pallas_call | solution.py:708

commit v3 on v2

--- a/solution.py
+++ b/solution.py
@@ -101,9 +101,9 @@
     dv_ref,
     drows_ref,
     dgates_ref,
-    gg_hbm,
-    gu_hbm,
-    gd_hbm,
+    out_a,
+    out_b,
+    out_d,
     kv_own,
     kvb,
     dkb,
@@ -135,11 +135,7 @@
     act_u,
     gub,
     hb,
-    out_a,
-    out_b,
-    out_d,
     w_sem,
-    out_sem,
     kv_sem,
     q_sem,
     a_sem,
@@ -258,13 +254,13 @@
             device_id_type=MESH,
         ).start()
 
-    def send_all(chunks, got, sems):
+    def send_all(chunks, got, sems, first=1, last=DEVS):
         def send(step, carry):
             pc, pk = any_partner(step, c, k)
             send_to(pc, pk, chunks, got, sems)
             return carry
 
-        lax.fori_loop(1, DEVS, send, 0)
+        lax.fori_loop(first, last, send, 0)
 
     def wait_all(buf, sem, count):
         part = buf.at[pl.ds(0, count)]
@@ -304,7 +300,7 @@
         return carry
 
     lax.fori_loop(1, 8, send_kv, 0)
-    send_all(send_a, recv_a, a_sem)
+    send_all(send_a, recv_a, a_sem, 1, 17)
     recv_a[pl.ds(me, 1)] = send_a[pl.ds(me, 1)]
     kvb[pl.ds(chip, 1)] = kv_own[...].reshape(1, 2, HALF, 256)
     wait_all(kvb, kv_sem.at[1], 7)
@@ -324,6 +320,7 @@
         return carry
 
     lax.fori_loop(0, 24, pass_kv, 0)
+    send_all(send_a, recv_a, a_sem, 17, DEVS)
 
     gather(mgrad_ref, gtable, yb, send_b)
     send_all(send_b, recv_b, b_sem)
@@ -460,8 +457,6 @@
         gt_send[h * HALF : (h + 1) * HALF] = jnp.broadcast_to(
             tile[:, None, :], (HALF, 16, 128)
         ).astype(BF16)
-    send_all(gt_send, gt_recv, gt_sem)
-    gt_recv[pl.ds(me, 1)] = gt_send[pl.ds(me, 1)]
 
     for h in range(2):
         span = slice(h * 320, (h + 1) * 320)
@@ -492,6 +487,8 @@
 
         lax.fori_loop(1, 64, send_half, 0)
     back[pl.ds(me, 1)] = send_a[pl.ds(me, 1)]
+    send_all(gt_send, gt_recv, gt_sem)
+    gt_recv[pl.ds(me, 1)] = gt_send[pl.ds(me, 1)]
 
     wait_all(rs1, rs_sem.at[1], 24)
 
@@ -512,20 +509,12 @@
         return carry
 
     lax.fori_loop(0, 8, grad_in, 0)
-    outs = [
-        pltpu.make_async_copy(src, dst, out_sem.at[i])
-        for i, (src, dst) in enumerate(((out_a, gg_hbm), (out_b, gu_hbm), (out_d, gd_hbm)))
-    ]
-    outs[0].start()
-    outs[1].start()
-
     def grad_out(n, carry):
         cols = pl.ds(pl.multiple_of(n * 512, 512), 512)
         out_d[:, cols] = dot_tn(hb[...], yb[:, cols]).astype(BF16)
         return carry
 
     lax.fori_loop(0, 4, grad_out, 0)
-    outs[2].start()
 
     wait_all(rs1, rs_sem.at[0], 24)
     wait_all(rs2, rs_sem.at[2], 7)
@@ -568,36 +557,14 @@
         return carry
 
     lax.fori_loop(0, 4, combine, 0)
-    for copy in outs:
+
+
+def hand_over(*refs):
+    copies = [pltpu.make_async_copy(refs[i], refs[8 + i], refs[16].at[i]) for i in range(8)]
+    for copy in reversed(copies):
+        copy.start()
+    for copy in copies:
         copy.wait()
-
-
-def hand_over(*refs):
-    small, big = refs[0:5], refs[5:8]
-    small_out, big_out = refs[8:13], refs[13:16]
-    held, in_sem, out_sem = refs[16:19], refs[19], refs[20]
-    steps = []
-    for i in range(3):
-        count = 4
-        depth = big[i].shape[0] // count
-        for part in range(count):
-            rows = pl.ds(part * depth, depth)
-            sem = i * count + part
-            steps.append(
-                (
-                    pltpu.make_async_copy(big[i].at[rows], held[i].at[rows], in_sem.at[sem]),
-                    pltpu.make_async_copy(held[i].at[rows], big_out[i].at[rows], out_sem.at[sem]),
-                )
-            )
-    for fetch, _ in steps:
-        fetch.start()
-    for src, dst in zip(small, small_out):
-        dst[...] = src[...]
-    for fetch, store in steps:
-        fetch.wait()
-        store.start()
-    for _, store in steps:
-        store.wait()
 
 
 def shards(
@@ -637,9 +604,9 @@
     )
     results = pl.pallas_call(
         layer_kernel,
-        out_shape=shapes,
+        out_shape=tuple(pltpu.VMEM(shape.shape, BF16) for shape in shapes),
         in_specs=[vmem] * 6 + [smem] + [vmem] * 4 + [hbm] * 3,
-        out_specs=(vmem,) * 5 + (hbm,) * 3,
+        out_specs=(vmem,) * 8,
         scratch_shapes=[
             pltpu.VMEM((2, HALF, 256), BF16),
             pltpu.VMEM((CHIPS, 2, HALF, 256), BF16),
@@ -672,10 +639,6 @@
             pltpu.VMEM((slots, hidden), F32),
             pltpu.VMEM((slots, 2 * hidden), BF16),
             pltpu.VMEM((slots, hidden), BF16),
-            pltpu.VMEM((width, hidden), BF16),
-            pltpu.VMEM((width, hidden), BF16),
-            pltpu.VMEM((hidden, width), BF16),
-            pltpu.SemaphoreType.DMA((3,)),
             pltpu.SemaphoreType.DMA((3,)),
             pltpu.SemaphoreType.DMA((4,)),
             pltpu.SemaphoreType.DMA((6,)),
@@ -687,7 +650,7 @@
             pltpu.SemaphoreType.DMA((2,)),
         ],
         compiler_params=pltpu.CompilerParams(
-            collective_id=0, has_side_effects=True, vmem_limit_bytes=62 * 1024 * 1024
+            collective_id=0, has_side_effects=True, vmem_limit_bytes=52 * 1024 * 1024
         ),
     )(
         query_rows.reshape(flat, size),
@@ -708,11 +671,10 @@
     results = pl.pallas_call(
         hand_over,
         out_shape=shapes,
-        in_specs=[vmem] * 5 + [hbm] * 3,
-        out_specs=(vmem,) * 5 + (hbm,) * 3,
-        scratch_shapes=[pltpu.VMEM(shape.shape, BF16) for shape in shapes[5:8]]
-        + [pltpu.SemaphoreType.DMA((12,))] * 2,
-        compiler_params=pltpu.CompilerParams(vmem_limit_bytes=60 * 1024 * 1024),
+        in_specs=[hbm] * 8,
+        out_specs=(hbm,) * 8,
+        scratch_shapes=[pltpu.SemaphoreType.DMA((8,))],
+        compiler_params=pltpu.CompilerParams(vmem_limit_bytes=16 * 1024 * 1024),
     )(*results)
     d_query, d_key, d_value, d_rows, d_gates, grad_gate, grad_up, grad_down = results
     return (

time: 186 us -> 167 us (0.90); the launches traced: 183 us -> 167 us
  Pallas kernels: 182 us -> 166 us
    pallas_call x2, Pallas kernels: 182 us -> 166 us  [the longest x1 162 us: shards(): pl.pallas_call(layer_kernel, out_shape=tuple((pltpu.VMEM(shape.shape, BF1...]
where the time goes in v3:
time: 167 us
  Pallas kernels  166 us (99%)
    pallas_call x1, Pallas kernels, shards(): pl.pallas_call(layer_kernel, out_shape=tuple((pltpu.VMEM(shape.shape, BF1...  162 us
    pallas_call x1, Pallas kernels, shards(): pl.pallas_call(hand_over, out_shape=shapes, in_specs=[hbm] * 8, out_specs...  3.91 us

profile of v3, /device:TPU:21, one launch (start us, length us, event | category | flops | bytes accessed | tf_op | source)
XLA Modules:
  0.0 167.0 jit_solution(1699982840925138415)
XLA Ops:
  0.6 162.4 %shard_map.197 = (bf16[1024,128]{1,0:T(8,128)(2,1)S(1)}, bf16[128,128]{1,0:T(8,128)(2,1)S(1)}, bf16[128,128]{1,0:T(8,128)(2,1)S(1)}, bf16[64,2048]{1,0:T(8,128)(...) custom-call(bf16[1024,128]{1,0:T(8,128)(2,1)} %bitcast.21, ...), custom_call_target="tpu_custom_call" | custom-call | tf_op jit(solution)/shard_map/pallas_call | solution.py:605
  163.1 3.9 %shard_map.198 = (bf16[1024,128]{1,0:T(8,128)(2,1)}, bf16[128,128]{1,0:T(8,128)(2,1)}, bf16[128,128]{1,0:T(8,128)(2,1)}, bf16[64,2048]{1,0:T(8,128)(2,1)}, bf16[...) custom-call(bf16[1024,128]{1,0:T(8,128)(2,1)S(1)} %get-tuple-element.24.ref, ...), custom_call_target="tpu_custom_call" | custom-call | tf_op jit(solution)/shard_map/pallas_call | solution.py:671

commit v4 on v3

--- a/solution.py
+++ b/solution.py
@@ -123,8 +123,6 @@
     recv_a,
     recv_b,
     back,
-    gt_send,
-    gt_recv,
     xb,
     yb,
     slb,
@@ -143,7 +141,6 @@
     rs_sem,
     dq_sem,
     ret_sem,
-    gt_sem,
 ):
     c = lax.axis_index("ctx")
     k = lax.axis_index("kv")
@@ -246,7 +243,7 @@
 
     def send_to(pc, pk, chunks, got, sems):
         pltpu.make_async_remote_copy(
-            src_ref=chunks.at[place(pc, pk)],
+            src_ref=chunks.at[place(pc, pk), pl.ds(0, CAP)],
             dst_ref=got.at[me],
             send_sem=sems.at[0],
             recv_sem=sems.at[1],
@@ -261,6 +258,22 @@
             return carry
 
         lax.fori_loop(first, last, send, 0)
+
+    def send_group(group, chunks, got, send_sem, recv_sem):
+        def send(step, carry):
+            chip_to, pk = chip_step(step, c, k)
+            pc = chip_to * 2 + lax.rem(core + group, 2)
+            pltpu.make_async_remote_copy(
+                src_ref=chunks.at[place(pc, pk)],
+                dst_ref=got.at[me],
+                send_sem=send_sem,
+                recv_sem=recv_sem,
+                device_id=(pc, pk),
+                device_id_type=MESH,
+            ).start()
+            return carry
+
+        lax.fori_loop(1 - group, 64, send, 0)
 
     def wait_all(buf, sem, count):
         part = buf.at[pl.ds(0, count)]
@@ -301,7 +314,7 @@
 
     lax.fori_loop(1, 8, send_kv, 0)
     send_all(send_a, recv_a, a_sem, 1, 17)
-    recv_a[pl.ds(me, 1)] = send_a[pl.ds(me, 1)]
+    recv_a[pl.ds(me, 1)] = send_a[pl.ds(me, 1), 0:CAP]
     kvb[pl.ds(chip, 1)] = kv_own[...].reshape(1, 2, HALF, 256)
     wait_all(kvb, kv_sem.at[1], 7)
 
@@ -323,8 +336,8 @@
     send_all(send_a, recv_a, a_sem, 17, DEVS)
 
     gather(mgrad_ref, gtable, yb, send_b)
-    send_all(send_b, recv_b, b_sem)
     recv_b[pl.ds(me, 1)] = send_b[pl.ds(me, 1)]
+    send_group(0, send_b, recv_b, b_sem.at[0], b_sem.at[1])
 
     for copy in to_core:
         copy.wait()
@@ -370,7 +383,9 @@
             dkb[pl.ds(i * 4, 4), late_key] = both.reshape(4, HALF, 256)
         return carry
 
-    lax.fori_loop(0, CHIPS // 4, key_tile, 0)
+    lax.fori_loop(0, 5, key_tile, 0)
+    send_group(1, send_b, recv_b, b_sem.at[0], b_sem.at[2])
+    lax.fori_loop(5, CHIPS // 4, key_tile, 0)
 
     dq_copy = pltpu.make_async_remote_copy(
         src_ref=dqs.at[1],
@@ -408,15 +423,15 @@
         ).start()
         return carry
 
-    def unpack(chunks, flat):
+    def unpack(chunks, flat, first, last):
         def body(block, carry):
             unpack_block(block, perm_ref[...], chunks, flat)
             return carry
 
-        lax.fori_loop(0, 8, body, 0)
+        lax.fori_loop(first, last, body, 0)
 
     wait_all(recv_a, a_sem.at[1], DEVS - 1)
-    unpack(recv_a, xb)
+    unpack(recv_a, xb, 0, 8)
     weights[0].wait()
     weights[1].wait()
 
@@ -428,38 +443,33 @@
 
     lax.fori_loop(0, 3, gate_up, 0)
     weights[2].wait()
-    wait_all(send_a, a_sem.at[0], DEVS - 1)
-    wait_all(recv_b, b_sem.at[1], DEVS - 1)
-    lax.fori_loop(0, 24, send_partial, 0)
-    unpack(recv_b, yb)
-
-    def hidden_part(n, gate_sum):
-        cols = pl.ds(pl.multiple_of(n * 256, 256), 256)
-        cols_up = pl.ds(pl.multiple_of(n * 256 + 768, 256), 256)
-        projected = dot_nt(yb[...], wd[cols, :])
-        ga = act_g[:, cols]
-        ua = act_u[:, cols]
-        sig = jax.nn.sigmoid(ga)
-        silu = ga * sig
-        hidden = (silu * ua).astype(BF16)
-        hb[:, cols] = hidden
-        gub[:, cols] = (projected * ua * sig * (1.0 + ga * (1.0 - sig))).astype(BF16)
-        gub[:, cols_up] = (projected * silu).astype(BF16)
-        return gate_sum + jnp.sum(projected * hidden.astype(F32), axis=1, keepdims=True)
-
-    gate_sum = lax.fori_loop(0, 3, hidden_part, jnp.zeros((640, 1), F32))
-    lane_h = lax.broadcasted_iota(jnp.int32, (HALF, 128), 1)
-    for h in range(2):
-        tile = jnp.zeros((HALF, 128), F32)
-        for r in range(CAP):
-            first = h * 320 + r * 64
-            tile = jnp.where(lane_h == r, gate_sum[first : first + 64], tile)
-        gt_send[h * HALF : (h + 1) * HALF] = jnp.broadcast_to(
-            tile[:, None, :], (HALF, 16, 128)
-        ).astype(BF16)
-
-    for h in range(2):
-        span = slice(h * 320, (h + 1) * 320)
+    dq_copy.wait()
+    dq_ref[...] = jnp.transpose((dqs[0] + dqr[...]) * score_scale).astype(BF16)
+    wait_all(recv_a, a_sem.at[0], DEVS - 1)
+
+    for group in range(2):
+        half = lax.rem(core + group, 2)
+        span = pl.ds(pl.multiple_of(half * 320, 64), 320)
+        wait_all(recv_b, b_sem.at[1 + group], 63 + group)
+        if group == 0:
+            lax.fori_loop(0, 24, send_partial, 0)
+        unpack(recv_b, yb, half * 4, half * 4 + 4)
+
+        def hidden_part(n, gate_sum):
+            cols = pl.ds(pl.multiple_of(n * 256, 256), 256)
+            cols_up = pl.ds(pl.multiple_of(n * 256 + 768, 256), 256)
+            projected = dot_nt(yb[span, :], wd[cols, :])
+            ga = act_g[span, cols]
+            ua = act_u[span, cols]
+            sig = jax.nn.sigmoid(ga)
+            silu = ga * sig
+            hidden = (silu * ua).astype(BF16)
+            hb[span, cols] = hidden
+            gub[span, cols] = (projected * ua * sig * (1.0 + ga * (1.0 - sig))).astype(BF16)
+            gub[span, cols_up] = (projected * silu).astype(BF16)
+            return gate_sum + jnp.sum(projected * hidden.astype(F32), axis=1, keepdims=True)
+
+        gate_sum = lax.fori_loop(0, 3, hidden_part, jnp.zeros((320, 1), F32))
 
         def slot_cols(n, carry):
             cols = pl.ds(pl.multiple_of(n * 256, 256), 256)
@@ -474,21 +484,18 @@
             pack_block(block, perm_ref[...], slb, send_a)
             return carry
 
-        lax.fori_loop(h * 4, h * 4 + 4, pack_back, 0)
-
-        @pl.when(core != h)
-        def _():
-            send_to(chip * 2 + h, k, send_a, back, ret_sem)
-
-        def send_half(step, carry):
-            pc, pk = chip_step(step, c, k)
-            send_to(pc * 2 + h, pk, send_a, back, ret_sem)
-            return carry
-
-        lax.fori_loop(1, 64, send_half, 0)
-    back[pl.ds(me, 1)] = send_a[pl.ds(me, 1)]
-    send_all(gt_send, gt_recv, gt_sem)
-    gt_recv[pl.ds(me, 1)] = gt_send[pl.ds(me, 1)]
+        lax.fori_loop(half * 4, half * 4 + 4, pack_back, 0)
+        lane_h = lax.broadcasted_iota(jnp.int32, (HALF, 128), 1)
+        tile = jnp.zeros((HALF, 128), F32)
+        for r in range(CAP):
+            tile = jnp.where(lane_h == r, gate_sum[r * 64 : r * 64 + 64], tile)
+        send_a[pl.ds(pl.multiple_of(half * HALF, HALF), HALF), CAP] = jnp.broadcast_to(
+            tile[:, None, :], (HALF, 16, 128)
+        ).astype(BF16)
+        send_group(group, send_a, back, ret_sem.at[0], ret_sem.at[1 + group])
+
+        if group == 0:
+            back[pl.ds(me, 1)] = send_a[pl.ds(me, 1)]
 
     wait_all(rs1, rs_sem.at[1], 24)
 
@@ -525,31 +532,28 @@
     for h in range(2):
         dk_ref[h * HALF : (h + 1) * HALF, :] = total[h, :, 0:128].astype(BF16)
         dv_ref[h * HALF : (h + 1) * HALF, :] = total[h, :, 128:256].astype(BF16)
-    dq_copy.wait()
-    dq_ref[...] = jnp.transpose((dqs[0] + dqr[...]) * score_scale).astype(BF16)
-
-    wait_all(gt_send, gt_sem.at[0], DEVS - 1)
-    wait_all(gt_recv, gt_sem.at[1], DEVS - 1)
-    slot_gates = gt_recv[...].astype(F32)[:, 0, :]
-    halves = []
-    for h in range(2):
-        acc = jnp.zeros((64, HALF), F32)
-        for r in range(CAP):
-            first = h * 320 + r * 64
-            acc = acc + table[first : first + 64, :].astype(F32) * slot_gates[
-                h * 64 : (h + 1) * 64, r : r + 1
-            ]
-        halves.append(acc)
-    gate_grads = jnp.concatenate(halves, axis=0)
-    for j in range(8):
-        dgates_ref[j : j + 1, :] = (
-            jnp.sum(hit(j) * gate_grads, axis=0, keepdims=True) / gates[j : j + 1, :]
-        ).astype(BF16)
 
     wait_all(send_b, b_sem.at[0], DEVS - 1)
     wait_all(send_a, ret_sem.at[0], DEVS - 1)
-    wait_all(back, ret_sem.at[1], DEVS - 1)
-    unpack(back, slb)
+    near_spot = lax.broadcasted_iota(jnp.int32, (HALF, HALF), 0)
+    gate_rows = [jnp.zeros((1, HALF), F32)] * 8
+    for group in range(2):
+        half = lax.rem(core + group, 2)
+        wait_all(back, ret_sem.at[1 + group], 63 + group)
+        unpack(back, slb, half * 4, half * 4 + 4)
+        slot_gates = back[pl.ds(half * HALF, HALF), CAP].astype(F32)[:, 0, :]
+        acc = jnp.zeros((HALF, HALF), F32)
+        for r in range(CAP):
+            first = pl.multiple_of(half * 320 + r * 64, 64)
+            acc = acc + table[pl.ds(first, 64), :].astype(F32) * slot_gates[:, r : r + 1]
+        owner = (near_spot // 2) * 4 + half * 2 + lax.rem(near_spot, 2)
+        for j in range(8):
+            named_here = owner == ids_ref[j : j + 1, :]
+            gate_rows[j] = gate_rows[j] + jnp.sum(
+                jnp.where(named_here, acc, 0.0), axis=0, keepdims=True
+            )
+    for j in range(8):
+        dgates_ref[j : j + 1, :] = (gate_rows[j] / gates[j : j + 1, :]).astype(BF16)
 
     def combine(n, carry):
         cols = pl.ds(pl.multiple_of(n * 512, 512), 512)
@@ -591,6 +595,7 @@
     smem = pl.BlockSpec(memory_space=pltpu.SMEM)
     hbm = pl.BlockSpec(memory_space=pl.ANY)
     chunk = (DEVS, CAP, TILES, 128)
+    chunk_and_gates = (DEVS, CAP + 1, TILES, 128)
     slots = DEVS * CAP
     shapes = (
         jax.ShapeDtypeStruct((flat, size), BF16),
@@ -622,13 +627,11 @@
             pltpu.VMEM((2, size, flat), F32),
             pltpu.VMEM((size, flat), F32),
             pltpu.VMEM((256, 256), BF16),
+            pltpu.VMEM(chunk_and_gates, BF16),
             pltpu.VMEM(chunk, BF16),
             pltpu.VMEM(chunk, BF16),
             pltpu.VMEM(chunk, BF16),
-            pltpu.VMEM(chunk, BF16),
-            pltpu.VMEM(chunk, BF16),
-            pltpu.VMEM((DEVS, 16, 128), BF16),
-            pltpu.VMEM((DEVS, 16, 128), BF16),
+            pltpu.VMEM(chunk_and_gates, BF16),
             pltpu.VMEM((slots, width), BF16),
             pltpu.VMEM((slots, width), BF16),
             pltpu.VMEM((slots, width), BF16),
@@ -643,11 +646,10 @@
             pltpu.SemaphoreType.DMA((4,)),
             pltpu.SemaphoreType.DMA((6,)),
             pltpu.SemaphoreType.DMA((2,)),
-            pltpu.SemaphoreType.DMA((2,)),
+            pltpu.SemaphoreType.DMA((3,)),
             pltpu.SemaphoreType.DMA((4,)),
             pltpu.SemaphoreType.DMA((2,)),
-            pltpu.SemaphoreType.DMA((2,)),
-            pltpu.SemaphoreType.DMA((2,)),
+            pltpu.SemaphoreType.DMA((3,)),
         ],
         compiler_params=pltpu.CompilerParams(
             collective_id=0, has_side_effects=True, vmem_limit_bytes=52 * 1024 * 1024

time: 167 us -> 160 us (0.958); the launches traced: 167 us -> 158 us
  Pallas kernels: 166 us -> 157 us
    pallas_call x1, Pallas kernels: 162 us -> 153 us  [shards(): pl.pallas_call(layer_kernel, out_shape=tuple((pltpu.VMEM(shape.shape, BF1...]
where the time goes in v4:
time: 160 us; the launch traced here: 158 us
  Pallas kernels  157 us (98%)
    pallas_call x1, Pallas kernels, shards(): pl.pallas_call(layer_kernel, out_shape=tuple((pltpu.VMEM(shape.shape, BF1...  153 us
    pallas_call x1, Pallas kernels, shards(): pl.pallas_call(hand_over, out_shape=shapes, in_specs=[hbm] * 8, out_specs...  3.91 us

profile of v4, /device:TPU:21, one launch (start us, length us, event | category | flops | bytes accessed | tf_op | source)
XLA Modules:
  0.0 158.0 jit_solution(17736199224397602993)
XLA Ops:
  0.6 153.4 %shard_map.197 = (bf16[1024,128]{1,0:T(8,128)(2,1)S(1)}, bf16[128,128]{1,0:T(8,128)(2,1)S(1)}, bf16[128,128]{1,0:T(8,128)(2,1)S(1)}, bf16[64,2048]{1,0:T(8,128)(...) custom-call(bf16[1024,128]{1,0:T(8,128)(2,1)} %bitcast.21, ...), custom_call_target="tpu_custom_call" | custom-call | tf_op jit(solution)/shard_map/pallas_call | solution.py:610
  154.1 3.9 %shard_map.198 = (bf16[1024,128]{1,0:T(8,128)(2,1)}, bf16[128,128]{1,0:T(8,128)(2,1)}, bf16[128,128]{1,0:T(8,128)(2,1)}, bf16[64,2048]{1,0:T(8,128)(2,1)}, bf16[...) custom-call(bf16[1024,128]{1,0:T(8,128)(2,1)S(1)} %get-tuple-element.24.ref, ...), custom_call_target="tpu_custom_call" | custom-call | tf_op jit(solution)/shard_map/pallas_call | solution.py:673

commit v5 on v4

--- a/solution.py
+++ b/solution.py
@@ -447,9 +447,20 @@
     dq_ref[...] = jnp.transpose((dqs[0] + dqr[...]) * score_scale).astype(BF16)
     wait_all(recv_a, a_sem.at[0], DEVS - 1)
 
+    def line_sum(i, carry):
+        own = dkb[at_b * step_b + (i // 2) * step_m + lax.rem(i, 2)].astype(F32)
+        for s in range(3):
+            own = own + rs1[s * 8 + i].astype(F32)
+        mid[i] = own.astype(BF16)
+        return carry
+
     for group in range(2):
         half = lax.rem(core + group, 2)
         span = pl.ds(pl.multiple_of(half * 320, 64), 320)
+        if group == 1:
+            wait_all(rs1, rs_sem.at[1], 24)
+            lax.fori_loop(0, 8, line_sum, 0)
+            lax.fori_loop(1, 8, send_mid, 0)
         wait_all(recv_b, b_sem.at[1 + group], 63 + group)
         if group == 0:
             lax.fori_loop(0, 24, send_partial, 0)
@@ -496,18 +507,6 @@
 
         if group == 0:
             back[pl.ds(me, 1)] = send_a[pl.ds(me, 1)]
-
-    wait_all(rs1, rs_sem.at[1], 24)
-
-    def line_sum(i, carry):
-        own = dkb[at_b * step_b + (i // 2) * step_m + lax.rem(i, 2)].astype(F32)
-        for s in range(3):
-            own = own + rs1[s * 8 + i].astype(F32)
-        mid[i] = own.astype(BF16)
-        return carry
-
-    lax.fori_loop(0, 8, line_sum, 0)
-    lax.fori_loop(1, 8, send_mid, 0)
 
     def grad_in(n, carry):
         rows = pl.ds(pl.multiple_of(n * 256, 256), 256)

time: 160 us -> 168 us (1.050)
  Pallas kernels: 157 us -> 167 us
    pallas_call x1, Pallas kernels: 153 us -> 163 us  [shards(): pl.pallas_call(layer_kernel, out_shape=tuple((pltpu.VMEM(shape.shape, BF1...]
where the time goes in v5:
time: 168 us; the launch traced here: 167 us
  Pallas kernels  167 us (99%)
    pallas_call x1, Pallas kernels, shards(): pl.pallas_call(layer_kernel, out_shape=tuple((pltpu.VMEM(shape.shape, BF1...  163 us
    pallas_call x1, Pallas kernels, shards(): pl.pallas_call(hand_over, out_shape=shapes, in_specs=[hbm] * 8, out_specs...  3.91 us

profile of v5, /device:TPU:21, one launch (start us, length us, event | category | flops | bytes accessed | tf_op | source)
XLA Modules:
  0.0 167.5 jit_solution(2489412068593481788)
XLA Ops:
  0.6 162.9 %shard_map.197 = (bf16[1024,128]{1,0:T(8,128)(2,1)S(1)}, bf16[128,128]{1,0:T(8,128)(2,1)S(1)}, bf16[128,128]{1,0:T(8,128)(2,1)S(1)}, bf16[64,2048]{1,0:T(8,128)(...) custom-call(bf16[1024,128]{1,0:T(8,128)(2,1)} %bitcast.21, ...), custom_call_target="tpu_custom_call" | custom-call | tf_op jit(solution)/shard_map/pallas_call | solution.py:609
  163.6 3.9 %shard_map.198 = (bf16[1024,128]{1,0:T(8,128)(2,1)}, bf16[128,128]{1,0:T(8,128)(2,1)}, bf16[128,128]{1,0:T(8,128)(2,1)}, bf16[64,2048]{1,0:T(8,128)(2,1)}, bf16[...) custom-call(bf16[1024,128]{1,0:T(8,128)(2,1)S(1)} %get-tuple-element.24.ref, ...), custom_call_target="tpu_custom_call" | custom-call | tf_op jit(solution)/shard_map/pallas_call | solution.py:672
